TPU v7x, 256 devices: a whole 4x4x8 slice. The times are simulated.
256 devices in a mesh: pipe: 4 (over z_hi, core), dp: 16 (over y, x), tensor: 4 (over z_lo).
Axes of the slice: x: 4, y: 4, z: 8 (z_hi: 2, z_lo: 4; z = z_hi * 4 + z_lo), core: 2. Of those that a mesh axis runs over, the one named last changes fastest.
Arguments:
- section_input: bfloat16 [4, 1, 16, 128, 8192], P('pipe', None, 'dp'), may hold values from -60 to 60
- norm_gain: float32 [4, 8192], P('pipe'), may hold values from 0.1 to 1.9
- key_weight: bfloat16 [4, 8192, 512], P('pipe', None, 'tensor'), may hold values from -0.0625 to 0.0625
- value_weight: bfloat16 [4, 8192, 512], P('pipe', None, 'tensor'), may hold values from -0.0625 to 0.0625
- queries: bfloat16 [4, 1, 16, 128, 4096], P('pipe', None, 'dp', None, 'tensor'), may hold values from -4 to 4
- out_cotangent: bfloat16 [4, 1, 16, 128, 4096], P('pipe', None, 'dp', None, 'tensor'), may hold values from -6 to 6
- segment_ids: int32 [1, 16, 128], P(None, 'dp'), may hold values from 0 to 3, never falling along the last dimension, each value on 1 to 64 neighbouring positions
- upstream: bfloat16 [1, 16, 128, 8192], P(None, 'dp', 'tensor'), may hold values from -2 to 2
Outputs:
- section_cotangent: bfloat16 [4, 1, 16, 128, 8192], P('pipe', None, 'dp', 'tensor')
- query_cotangent: bfloat16 [4, 1, 16, 128, 4096], P('pipe', None, 'dp', None, 'tensor')
- key_weight_grad: float32 [4, 8192, 512], P('pipe', 'dp', 'tensor')
- value_weight_grad: float32 [4, 8192, 512], P('pipe', 'dp', 'tensor')
Inputs may be any that keep to these rules, and one draw needn't show every extreme that they name: `segment_ids`: ids never fall along a sequence and start at 0; one document has exactly 64 tokens in every sequence, none more.
All inputs are finite; a program needn't handle non-finite values.
Results may differ from a plain program's by a relative error of at most 0.019.
Values may be sent and summed in bfloat16 or wider, within the bound.
A program may use at most 128 MiB of HBM per device.

v0:
```python
import math

import jax
import jax.numpy as jnp
from jax import lax
from jax.sharding import PartitionSpec as P

NORM_EPS = 1e-05


def shifted(x, axis, by):
    peers = lax.axis_size(axis)
    pairs = [(i, i + by) for i in range(peers) if 0 <= i + by < peers]
    return lax.ppermute(x, axis, pairs)


def per_device(
    section_input,
    norm_gain,
    key_weight,
    value_weight,
    queries,
    out_cotangent,
    segment_ids,
    upstream,
):
    micro_count = section_input.shape[1]
    seq_len = section_input.shape[3]
    model_width = section_input.shape[4]
    head_size = key_weight.shape[2]
    group_size = queries.shape[4] // head_size
    inputs = section_input.reshape(micro_count, seq_len, model_width)
    gain_vec = norm_gain[0]
    key_mat = key_weight[0]
    value_mat = value_weight[0]
    query_all = queries.reshape(micro_count, seq_len, group_size, head_size)
    cot_all = out_cotangent.reshape(micro_count, seq_len, group_size, head_size)
    seg_all = segment_ids.reshape(micro_count, seq_len)
    factor = 1.0 / math.sqrt(head_size)
    places = jnp.arange(seq_len)

    def attend(items):
        rows_in, query_rows, cot_rows, seg_row = items
        input_f = rows_in.astype(jnp.float32)
        inverse = lax.rsqrt(jnp.mean(input_f * input_f, axis=-1, keepdims=True) + NORM_EPS)
        normed = (input_f * inverse * gain_vec).astype(jnp.bfloat16)
        keys = jnp.dot(normed, key_mat, preferred_element_type=jnp.float32).astype(jnp.bfloat16)
        values = jnp.dot(normed, value_mat, preferred_element_type=jnp.float32).astype(jnp.bfloat16)
        allowed = (places[None, :] <= places[:, None]) & (seg_row[:, None] == seg_row[None, :])
        scores = (
            jnp.einsum("igd,jd->gij", query_rows, keys, preferred_element_type=jnp.float32) * factor
        )
        weights = jnp.where(allowed, jnp.exp(scores), 0.0)
        probs = weights / jnp.sum(weights, axis=-1, keepdims=True)
        probs_low = probs.astype(jnp.bfloat16)
        dprob = jnp.einsum("igd,jd->gij", cot_rows, values, preferred_element_type=jnp.float32)
        inner = jnp.sum(probs * dprob, axis=-1, keepdims=True)
        dscore = (probs * (dprob - inner)).astype(jnp.bfloat16)
        query_grad = (
            jnp.einsum("gij,jd->igd", dscore, keys, preferred_element_type=jnp.float32) * factor
        ).astype(jnp.bfloat16)
        key_grad = (
            jnp.einsum("gij,igd->jd", dscore, query_rows, preferred_element_type=jnp.float32)
            * factor
        ).astype(jnp.bfloat16)
        value_grad = jnp.einsum(
            "gij,igd->jd", probs_low, cot_rows, preferred_element_type=jnp.float32
        ).astype(jnp.bfloat16)
        return (normed, query_grad, key_grad, value_grad)

    normed, query_grad, key_grad, value_grad = lax.map(
        attend, (inputs, query_all, cot_all, seg_all)
    )
    token_count = micro_count * seq_len
    normed_flat = normed.reshape(token_count, model_width)
    key_flat = key_grad.reshape(token_count, head_size)
    value_flat = value_grad.reshape(token_count, head_size)
    head_terms = jnp.dot(key_flat, key_mat.T, preferred_element_type=jnp.float32)
    head_terms = head_terms + jnp.dot(value_flat, value_mat.T, preferred_element_type=jnp.float32)
    head_low = head_terms.astype(jnp.bfloat16).reshape(micro_count, seq_len, model_width)
    normed_grad = lax.psum_scatter(head_low, "tensor", scatter_dimension=1, tiled=True).astype(
        jnp.float32
    )
    shard_rows = seq_len // lax.axis_size("tensor")
    own_rows = lax.dynamic_slice_in_dim(
        inputs, lax.axis_index("tensor") * shard_rows, shard_rows, 1
    ).astype(jnp.float32)
    own_inverse = lax.rsqrt(jnp.mean(own_rows * own_rows, axis=-1, keepdims=True) + NORM_EPS)
    unit_rows = own_rows * own_inverse
    upper = normed_grad * gain_vec
    contribution = own_inverse * (
        upper - unit_rows * jnp.mean(upper * unit_rows, axis=-1, keepdims=True)
    )
    suffix = contribution
    for section_hop in range(lax.axis_size("pipe") - 1):
        suffix = contribution + shifted(suffix.astype(jnp.bfloat16), "pipe", -1).astype(
            suffix.dtype
        )
    totals = upstream.reshape(micro_count, shard_rows, model_width).astype(jnp.float32) + suffix
    section_cotangent = totals.astype(jnp.bfloat16).reshape(
        1, micro_count, 1, shard_rows, model_width
    )
    key_wgrad = jnp.dot(normed_flat.T, key_flat, preferred_element_type=jnp.float32)
    value_wgrad = jnp.dot(normed_flat.T, value_flat, preferred_element_type=jnp.float32)
    key_wgrad, value_wgrad = (
        lax.psum_scatter(
            key_wgrad.astype(jnp.bfloat16), "dp", scatter_dimension=0, tiled=True
        ).astype(jnp.float32),
        lax.psum_scatter(
            value_wgrad.astype(jnp.bfloat16), "dp", scatter_dimension=0, tiled=True
        ).astype(jnp.float32),
    )
    query_cotangent = query_grad.reshape(1, micro_count, 1, seq_len, group_size * head_size)
    return (section_cotangent, query_cotangent, key_wgrad[None], value_wgrad[None])


def solution(mesh):
    return jax.shard_map(
        per_device,
        mesh=mesh,
        in_specs=(
            P("pipe", None, "dp", None, None),
            P("pipe", None),
            P("pipe", None, "tensor"),
            P("pipe", None, "tensor"),
            P("pipe", None, "dp", None, "tensor"),
            P("pipe", None, "dp", None, "tensor"),
            P(None, "dp", None),
            P(None, "dp", "tensor", None),
        ),
        out_specs=(
            P("pipe", None, "dp", "tensor", None),
            P("pipe", None, "dp", None, "tensor"),
            P("pipe", "dp", "tensor"),
            P("pipe", "dp", "tensor"),
        ),
        check_vma=False,
    )
```

profile of v0, /device:TPU:32, one launch (start us, length us, event | category | flops | bytes accessed | tf_op | source)
XLA Modules:
  0.0 256.1 jit_solution(12501694575287360651)
XLA Ops:
  7.3 2.2 fusion.4
  9.7 0.1 fusion.58
  9.8 2.4 fusion.35
  12.2 3.4 %convolution_bitcast_fusion = f32[8,128,128]{1,2,0:T(8,128)} fusion(bf16[1,8192,128]{2,1,0:T(8,128)(2,1)S(1)} %copy-done, bf16[1,1,1,128,8192]{4,3,2,1,0:T(8,128)(2,1)} %param.8, f32[8192]{0:T(1024)S(1)} %bitcast.116, f32[128]{0:T(128)S(1)} %add_rsqrt_fusion, bf16[128,8,128]{2,1,0:T(8,128)(2,1)S(1)} %bitcast.130), kind=kOutput, calls=%fused_computation.27 | convolution fusion | flops 306200576 | bytes 5014016 | tf_op jit(solution)/shard_map/while/body/eval_jaxpr/igd,jd->gij/dot_general | solution.py:56
  15.6 0.2 fusion.21
  15.9 2.2 multiply_reduce_fusion
  18.0 1.3 multiply_convert_fusion
  19.3 0.2 fusion.31
  19.5 4.2 %fusion.13 = f32[128,8192]{1,0:T(8,128)} fusion(bf16[128,128]{1,0:T(8,128)(2,1)S(1)} %fusion.31, bf16[1,8192,128]{2,1,0:T(8,128)(2,1)} %param.10), kind=kOutput, calls=%fused_computation.18 | convolution fusion | flops 268435456 | bytes 6324224 | tf_op jit(solution)/shard_map/dot_general | solution.py:78
  23.7 0.3 fusion.24
  24.0 4.2 %fusion.1 = bf16[1,128,8192]{2,1,0:T(8,128)(2,1)} fusion(f32[128,8192]{1,0:T(8,128)} %fusion.13, bf16[128,128]{1,0:T(8,128)(2,1)S(1)} %fusion.24, bf16[1,8192,128]{2,1,0:T(8,128)(2,1)S(1)} %copy-done), kind=kOutput, calls=%fused_computation.4 | convolution fusion | flops 270532608 | bytes 8421376 | tf_op jit(solution)/shard_map/dot_general | solution.py:79
  28.3 3.8 %convolution_convert_fusion.1 = bf16[8192,128]{1,0:T(8,128)(2,1)} fusion(bf16[128,128]{1,0:T(8,128)(2,1)S(1)} %fusion.31, bf16[1,1,1,128,8192]{4,3,2,1,0:T(8,128)(2,1)} %param.8, f32[8192]{0:T(1024)S(1)} %bitcast.117, f32[128]{0:T(128)S(1)} %add_rsqrt_fusion), kind=kOutput, calls=%fused_computation.3 | convolution fusion | flops 273678336 | bytes 4260352 | tf_op jit(solution)/shard_map/dot_general | solution.py:103
  32.2 1.3 fusion.41
  33.4 44.3 %reduce-scatter.4.cloned.1.call-done = bf16[1,32,8192]{2,1,0:T(8,128)(2,1)} async-done(((bf16[1,128,8192]{2,1,0:T(8,128)(2,1)}), bf16[1,32,8192]{2,1,0:T(8,128)(2,1)}) %reduce-scatter.4.cloned.1.call-update) | async-done | bytes 524304 | tf_op jit(solution)/shard_map/reduce_scatter | solution.py:81
  77.7 1.7 fusion.38
  79.4 1.5 fusion.64
  80.9 1.3 collective-permute-start
  82.2 2.2 convolution_convert_fusion
  84.4 0.4 collective-permute-done
  84.9 0.6 copy-done.3
  85.4 1.6 add_convert_fusion.1
  87.0 1.3 collective-permute-start.1
  88.3 17.3 %collective-permute-done.1 = bf16[1,32,8192]{2,1,0:T(8,128)(2,1)S(1)} collective-permute-done((bf16[1,32,8192]{2,1,0:T(8,128)(2,1)S(1)}, bf16[1,32,8192]{2,1,0:T(8,128)(2,1)S(1)}, u32[]{:S(2)}, u32[]{:S(2)}) %collective-permute-start.1) | collective-permute-done | bytes 524320 | tf_op jit(solution)/shard_map/ppermute | solution.py:14
  105.6 2.2 add_convert_fusion
  107.8 1.3 collective-permute-start.2
  109.1 0.2 fusion.22
  109.4 0.9 copy.18
  110.2 52.8 %reduce-scatter.6.cloned.1.call-done = bf16[512,128]{1,0:T(8,128)(2,1)} async-done(((bf16[8192,128]{1,0:T(8,128)(2,1)}), bf16[512,128]{1,0:T(8,128)(2,1)}) %reduce-scatter.6.cloned.1.call-update) | async-done | bytes 131088 | tf_op jit(solution)/shard_map/reduce_scatter | solution.py:106
  163.1 1.6 bitcast_convert_fusion.1
  164.7 80.7 %reduce-scatter.8.cloned.1.call-done = bf16[512,128]{1,0:T(8,128)(2,1)} async-done(((bf16[8192,128]{1,0:T(8,128)(2,1)}), bf16[512,128]{1,0:T(8,128)(2,1)}) %reduce-scatter.8.cloned.1.call-update) | async-done | bytes 131088 | tf_op jit(solution)/shard_map/reduce_scatter | solution.py:109
  245.4 1.6 bitcast_convert_fusion
  247.0 2.6 %fusion.50 = bf16[1,1,1,32,8192]{4,3,2,1,0:T(8,128)(2,1)} fusion(bf16[1,32,8192]{2,1,0:T(8,128)(2,1)} %collective-permute-done.2, bf16[1,1,32,8192]{3,2,1,0:T(8,128)(2,1)} %param.15, f32[32]{0:T(128)S(1)} %broadcast_multiply_fusion, bf16[1,1,1,128,8192]{4,3,2,1,0:T(8,128)(2,1)} %param.8, s32[]{:T(128)S(6)} %select_n.8, f32[8192]{0:T(1024)S(1)} %bitcast.123, ...), kind=kLoop, calls=%fused_computation.51 | loop fusion | flops 3145728 | bytes 2654468 | tf_op jit(solution)/shard_map/reshape | solution.py:100
  (27 shorter events, 0.3 us)
Async XLA Ops:
  7.2 5.1 %copy-start = (bf16[1,8192,128]{2,1,0:T(8,128)(2,1)S(1)}, bf16[1,8192,128]{2,1,0:T(8,128)(2,1)}, u32[]{:S(2)}) copy-start(bf16[1,8192,128]{2,1,0:T(8,128)(2,1)} %param.11) | copy-start | bytes 6291460
  7.2 2.3 copy-start.5
  7.2 2.4 copy-start.6
  7.2 2.4 copy-start.7
  7.2 2.5 copy-start.4
  7.2 70.5 %reduce-scatter.4.cloned.1.call-start = ((), (), s32[]{:S(2)}) async-start(), calls=%async_computation.3 | async-start | bytes 2621440 | tf_op jit(solution)/shard_map/reduce_scatter | solution.py:81
  7.3 2.5 copy-start.1
  28.3 134.8 %reduce-scatter.6.cloned.1.call-start = ((), (), s32[]{:S(2)}) async-start(), calls=%async_computation.4 | async-start | bytes 2228224 | tf_op jit(solution)/shard_map/reduce_scatter | solution.py:106
  32.1 213.3 %reduce-scatter.8.cloned.1.call-start = ((), (), s32[]{:S(2)}) async-start(), calls=%async_computation.5 | async-start | bytes 2228224 | tf_op jit(solution)/shard_map/reduce_scatter | solution.py:109
  77.7 4.5 %copy-start.2 = (bf16[1,1,1,128,8192]{4,3,2,1,0:T(8,128)(2,1)S(1)}, bf16[1,1,1,128,8192]{4,3,2,1,0:T(8,128)(2,1)}, u32[]{:S(2)}) copy-start(bf16[1,1,1,128,8192]{4,3,2,1,0:T(8,128)(2,1)} %param.8) | copy-start | bytes 6291460
  80.9 3.9 %collective-permute-start = (bf16[1,32,8192]{2,1,0:T(8,128)(2,1)S(1)}, bf16[1,32,8192]{2,1,0:T(8,128)(2,1)}, u32[]{:S(2)}, u32[]{:S(2)}) collective-permute-start(bf16[1,32,8192]{2,1,0:T(8,128)(2,1)S(1)} %fusion.64), channel_id=1, source_target_pairs={{64,0},{128,64},{192,128},{65,1},{129,65},{193,129},{66,2},{130,66... | collective-permute-start | bytes 1572872 | tf_op jit(solution)/shard_map/ppermute | solution.py:14
  84.4 1.0 copy-start.3
  87.0 18.6 %collective-permute-start.1 = (bf16[1,32,8192]{2,1,0:T(8,128)(2,1)S(1)}, bf16[1,32,8192]{2,1,0:T(8,128)(2,1)S(1)}, u32[]{:S(2)}, u32[]{:S(2)}) collective-permute-start(bf16[1,32,8192]{2,1,0:T(8,128)(2,1)S(1)} %add_convert_fusion.1), channel_id=1, source_target_pairs={{64,0},{128,64},{192,128},{65,1},{129,65},{193,129},{66,2},{130,66... | collective-permute-start | bytes 1572872 | tf_op jit(solution)/shard_map/ppermute | solution.py:14
  107.8 139.2 %collective-permute-start.2 = (bf16[1,32,8192]{2,1,0:T(8,128)(2,1)}, bf16[1,32,8192]{2,1,0:T(8,128)(2,1)}, u32[]{:S(2)}, u32[]{:S(2)}) collective-permute-start(bf16[1,32,8192]{2,1,0:T(8,128)(2,1)} %add_convert_fusion), channel_id=1, source_target_pairs={{64,0},{128,64},{192,128},{65,1},{129,65},{193,129},{66,2},{130,66... | collective-permute-start | bytes 1572872 | tf_op jit(solution)/shard_map/ppermute | solution.py:14
Sparse Core Ops, SparseCore 0:
  28.4 49.3 reduce-scatter.3
  81.7 81.3 reduce-scatter.5
  166.6 78.7 reduce-scatter.7
where the time goes:
time: 257 us; the launch traced here: 256 us
  waiting for transfers between devices  196 us (76%)
  matrix products  23.3 us (9%)
  other arithmetic  17.6 us (7%)
  between operations  14 us (5%)
  starting transfers between devices  3.99 us (2%)
    reduce_scatter x1, waiting for transfers between devices, per_device(): lax.psum_scatter(value_wgrad.astype(jnp.bfloat16), 'dp', scatter_dimensio...  80.7 us
    reduce_scatter x1, waiting for transfers between devices, per_device(): lax.psum_scatter(key_wgrad.astype(jnp.bfloat16), 'dp', scatter_dimension=...  52.8 us
    reduce_scatter x1, waiting for transfers between devices, per_device(): lax.psum_scatter(head_low, 'tensor', scatter_dimension=1, tiled=True)  44.3 us
    ppermute x3, waiting for transfers between devices, shifted(): return lax.ppermute(x, axis, pairs)  17.8 us
    convert_element_type x3, other arithmetic, per_device(): suffix.astype(jnp.bfloat16)  5.26 us
  transfers between devices with their start and end apart: 6, of which 5 were waited for; matrix products, arithmetic and copies ran while one was open for 7% of the time, Pallas kernels for 0%

commit v1 on v0

v1 whole, which is shorter than its diff:
```python
import functools
import math

import jax
import jax.numpy as jnp
from jax import lax
from jax.experimental import pallas as pl
from jax.experimental.pallas import tpu as pltpu
from jax.sharding import PartitionSpec as P

NORM_EPS = 1e-05
MESH = pl.DeviceIdType.MESH
F32 = jnp.float32
BF16 = jnp.bfloat16


def kernel(
    dims,
    x_hbm, gain_hbm, kw_hbm, vw_hbm, q_hbm, oc_hbm, seg_hbm, up_hbm,
    sc_out, dq_out, kg_out, vg_out,
    x_v, n_v, w_v, wg_v, q_v, oc_v, seg_v, up_v, gain_v, inv_v,
    nx_v, dq_v, dkv_v, mp_v, mr_v, ag_v, gs_v, gr_v, sr_v, sb_v, so_v,
    ps_v, pr_v, kg_v, vg_v,
    ld, wr, ws_s, ws_r, nx_s, nx_r, zk_s, zk_r, zm_s, zm_r,
    a1_s, a1_r, a2_s, a2_r, g_s, g_r, c_s, c_r, p_s, p_r,
):
    n_pipe, n_dp, n_t, side, seq, width, head, group = dims
    blk = width // n_dp
    quarter = seq // n_t
    two = 2 * head
    pipe = lax.axis_index("pipe")
    d = lax.axis_index("dp")
    t = lax.axis_index("tensor")
    mx = lax.rem(d, side)
    my = d // side

    def at_xy(dx, dy):
        return lax.rem(my + dy, side) * side + lax.rem(mx + dx, side)

    def at_z(dt):
        return lax.rem(t + dt, n_t)

    def local(src, dst, i):
        c = pltpu.make_async_copy(src, dst, ld.at[i])
        c.start()
        return c

    def remote(src, dst, ss, rs, i, dev):
        return pltpu.make_async_remote_copy(
            src_ref=src, dst_ref=dst, send_sem=ss.at[i], recv_sem=rs.at[i],
            device_id=dev, device_id_type=MESH,
        )

    offsets = [(dx, dy) for dy in range(side) for dx in range(side) if dx or dy]

    def dev_d(dd):
        return (pipe, dd, t)

    def dev_t(tt):
        return (pipe, d, tt)

    barrier = pltpu.get_barrier_semaphore()
    for dx, dy in offsets:
        pl.semaphore_signal(barrier, inc=1, device_id=dev_d(at_xy(dx, dy)), device_id_type=MESH)
    for dt in range(1, n_t):
        pl.semaphore_signal(barrier, inc=1, device_id=dev_t(at_z(dt)), device_id_type=MESH)
    for dp_ in range(1, n_pipe):
        pl.semaphore_signal(
            barrier, inc=1, device_id=(lax.rem(pipe + dp_, n_pipe), d, t), device_id_type=MESH
        )

    rows_d = pl.ds(pl.multiple_of(d * blk, blk), blk)
    wcol = pl.multiple_of(t * two, two)
    own_k = local(kw_hbm.at[rows_d], wg_v.at[:, pl.ds(wcol, head)], 0)
    own_v = local(vw_hbm.at[rows_d], wg_v.at[:, pl.ds(wcol + head, head)], 1)
    gain_c = local(gain_hbm, gain_v, 2)

    def rows_of(i):
        return pl.ds(pl.multiple_of(lax.rem(t + i, n_t) * quarter, quarter), quarter)

    x_cs = [local(x_hbm.at[rows_of(i)], x_v.at[rows_of(i)], 3 + i) for i in range(n_t)]
    n_w = 4
    wrows = width // n_w
    w_cs = []
    for i in range(n_w):
        r = pl.ds(i * wrows, wrows)
        w_cs.append(local(kw_hbm.at[r], w_v.at[r, pl.ds(0, head)], 7 + 2 * i))
        w_cs.append(local(vw_hbm.at[r], w_v.at[r, pl.ds(head, head)], 8 + 2 * i))
    seg_c = local(seg_hbm, seg_v, 15)
    q_c = local(q_hbm, q_v, 16)
    oc_c = local(oc_hbm, oc_v, 17)
    up_c = local(up_hbm, up_v, 18)

    step = 512

    def norm_quarter(i):
        r = rows_of(i)
        acc = jnp.zeros((quarter, 128), F32)
        for c in range(0, width, step):
            xf = x_v[r, c:c + step].astype(F32)
            sq = xf * xf
            for j in range(0, step, 128):
                acc = acc + sq[:, j:j + 128]
        mean = jnp.sum(acc, axis=-1, keepdims=True) * (1.0 / width)
        inv = lax.rsqrt(mean + NORM_EPS)
        for c in range(0, width, step):
            xf = x_v[r, c:c + step].astype(F32)
            n_v[r, c:c + step] = (xf * inv * gain_v[:, c:c + step]).astype(BF16)
        return inv

    gain_c.wait()
    x_cs[0].wait()
    inv_v[...] = jnp.broadcast_to(norm_quarter(0), (quarter, 128))
    own_k.wait()
    own_v.wait()
    pl.semaphore_wait(barrier, len(offsets) + n_t - 1 + n_pipe - 1)

    own_rows = rows_of(0)
    w_sends = []
    for dt in range(1, n_t):
        ref = wg_v.at[:, pl.ds(wcol, two)]
        c = remote(ref, ref, ws_s, ws_r, dt - 1, dev_t(at_z(dt)))
        c.start()
        w_sends.append(c)

    def blk_cols(dd):
        return pl.ds(pl.multiple_of(dd * blk, blk), blk)

    n_sends = []
    for i, (dx, dy) in enumerate(offsets):
        dd = at_xy(dx, dy)
        c = remote(n_v.at[own_rows, blk_cols(dd)], nx_v.at[d], nx_s, nx_r, i, dev_d(dd))
        c.start()
        n_sends.append(c)
    nx_v[d] = n_v[own_rows, blk_cols(d)]

    for i in range(1, n_t):
        x_cs[i].wait()
        norm_quarter(i)

    kv = jnp.zeros((seq, two), F32)
    for i in range(n_w):
        w_cs[2 * i].wait()
        w_cs[2 * i + 1].wait()
        kv = kv + jnp.dot(
            n_v[:, i * wrows:(i + 1) * wrows], w_v[i * wrows:(i + 1) * wrows, :],
            preferred_element_type=F32,
        )
    keys = kv[:, :head].astype(BF16)
    values = kv[:, head:].astype(BF16)

    factor = 1.0 / math.sqrt(head)
    seg_c.wait()
    seg_r = jnp.broadcast_to(seg_v[...], (seq, seq))
    ri = lax.broadcasted_iota(jnp.int32, (seq, seq), 0)
    ci = lax.broadcasted_iota(jnp.int32, (seq, seq), 1)
    allowed1 = (ci <= ri) & (seg_r == seg_r.T)
    allowed = jnp.concatenate([allowed1.astype(F32)] * group, axis=0) > 0.5
    q_c.wait()
    oc_c.wait()
    qs = jnp.concatenate([q_v[:, g * head:(g + 1) * head] for g in range(group)], axis=0)
    ocs = jnp.concatenate([oc_v[:, g * head:(g + 1) * head] for g in range(group)], axis=0)
    nt = (((1,), (1,)), ((), ()))
    tn = (((0,), (0,)), ((), ()))
    s = lax.dot_general(qs, keys, nt, preferred_element_type=F32) * factor
    dprob = lax.dot_general(ocs, values, nt, preferred_element_type=F32)
    e = jnp.where(allowed, jnp.exp(s), 0.0)
    probs = e / jnp.sum(e, axis=-1, keepdims=True)
    inner = jnp.sum(probs * dprob, axis=-1, keepdims=True)
    ds_ = (probs * (dprob - inner)).astype(BF16)
    pb = probs.astype(BF16)
    dk = (lax.dot_general(ds_, qs, tn, preferred_element_type=F32) * factor).astype(BF16)
    dv = lax.dot_general(pb, ocs, tn, preferred_element_type=F32).astype(BF16)
    dkv_v[:, :head] = dk
    dkv_v[:, head:] = dv
    msum = jnp.sum(
        dk.astype(F32) * kv[:, :head] + dv.astype(F32) * kv[:, head:], axis=-1, keepdims=True
    )
    mp_v[...] = jnp.broadcast_to(msum, (seq, 128))

    z_sends = []
    for dt in range(1, n_t):
        tt = at_z(dt)
        r = pl.ds(pl.multiple_of(tt * quarter, quarter), quarter)
        c1 = remote(dkv_v.at[r], ag_v.at[my, mx, :, pl.ds(wcol, two)], zk_s, zk_r, dt - 1, dev_t(tt))
        c1.start()
        c2 = remote(mp_v.at[r], mr_v.at[dt], zm_s, zm_r, dt - 1, dev_t(tt))
        c2.start()
        z_sends += [c1, c2]
    ag_v[my, mx, :, pl.ds(wcol, two)] = dkv_v[own_rows, :]
    mr_v[0] = mp_v[own_rows, :]

    dq = (jnp.dot(ds_, keys, preferred_element_type=F32) * factor).astype(BF16)
    for g in range(group):
        dq_v[:, g * head:(g + 1) * head] = dq[g * seq:(g + 1) * seq, :]
    dq_c = pltpu.make_async_copy(dq_v, dq_out, wr.at[0])
    dq_c.start()

    for c in z_sends:
        c.wait()

    half = two * n_t // 2
    p1 = []
    for i in range(1, side):
        ref = ag_v.at[my, mx, :, pl.ds(0, half)]
        c = remote(ref, ref, a1_s, a1_r, i - 1, dev_d(at_xy(i, 0)))
        c.start()
        p1.append(c)
    for i in range(1, side):
        ref = ag_v.at[my, mx, :, pl.ds(half, half)]
        c = remote(ref, ref, a1_s, a1_r, side - 1 + i - 1, dev_d(at_xy(0, i)))
        c.start()
        p1.append(c)
    for c in p1[:side - 1]:
        c.wait()
    p2 = []
    for i in range(1, side):
        ref = ag_v.at[my, :, :, pl.ds(0, half)]
        c = remote(ref, ref, a2_s, a2_r, i - 1, dev_d(at_xy(0, i)))
        c.start()
        p2.append(c)
    for c in p1[side - 1:]:
        c.wait()
    for i in range(1, side):
        ref = ag_v.at[:, mx, :, pl.ds(half, half)]
        c = remote(ref, ref, a2_s, a2_r, side - 1 + i - 1, dev_d(at_xy(i, 0)))
        c.start()
        p2.append(c)

    for c in n_sends:
        c.wait()
    for c in w_sends:
        c.wait()
    nxt = nx_v[...].reshape(n_dp * quarter, blk).T

    for c in p2:
        c.wait()

    g_sends = []
    gi = 0
    for k in range(side):
        yy = lax.rem(my + k, side)
        lhs = ag_v[yy].reshape(side * quarter, n_t * two)
        gk = lax.dot_general(lhs, wg_v[...], nt, preferred_element_type=F32).astype(BF16)
        gs_v[yy] = gk.reshape(side, quarter, blk)
        for dx in range(side):
            if k == 0 and dx == 0:
                continue
            dd = at_xy(dx, k)
            c = remote(
                gs_v.at[yy, lax.rem(mx + dx, side)], gr_v.at[:, blk_cols(d)],
                g_s, g_r, gi, dev_d(dd),
            )
            c.start()
            g_sends.append(c)
            gi += 1
        if k == 0:
            gr_v[:, blk_cols(d)] = gs_v[my, mx]

    full = ag_v[...].reshape(n_dp * quarter, n_t * two)
    part = jnp.dot(nxt, full, preferred_element_type=F32)
    for h in range(n_t):
        ps_v[h] = part[:, h * two:(h + 1) * two].astype(BF16)
    w_red = []
    for dt in range(1, n_t):
        tt = at_z(dt)
        c = remote(ps_v.at[tt], pr_v.at[dt - 1], p_s, p_r, dt - 1, dev_t(tt))
        c.start()
        w_red.append(c)

    up_c.wait()

    @pl.when(pipe == n_pipe - 1)
    def _():
        sr_v[...] = jnp.zeros(sr_v.shape, BF16)

    m = mr_v[0]
    for h in range(1, n_t):
        m = m + mr_v[h]
    m = m[:, :1] * (1.0 / width)
    inv = inv_v[:, :1]
    im = inv * inv * m
    prev = (lax.rem(pipe + n_pipe - 1, n_pipe), d, t)
    cw = side * blk
    outs = []
    chain = []
    gi = 0
    for k in range(side):
        yy = lax.rem(my + side - k, side)
        cols = pl.ds(pl.multiple_of(yy * cw, cw), cw)
        for dx in range(side):
            if k == 0 and dx == 0:
                continue
            g_sends[gi].wait_recv()
            gi += 1
        c = remote(sb_v.at[:, cols], sr_v.at[:, cols], c_s, c_r, k, prev)
        chain.append(c)

        @pl.when(pipe < n_pipe - 1)
        def _():
            c.wait_recv()

        for j in range(0, cw, step):
            cc = pl.ds(pl.multiple_of(yy * cw + j, step), step)
            gf = gr_v[:, cc].astype(F32)
            xf = x_v[own_rows, cc].astype(F32)
            con = inv * (gain_v[:, cc] * gf) - xf * im + sr_v[:, cc].astype(F32)
            sb_v[:, cc] = con.astype(BF16)
            so_v[:, cc] = (up_v[:, cc].astype(F32) + con).astype(BF16)

        @pl.when(pipe > 0)
        def _():
            c.start()

        o = pltpu.make_async_copy(so_v.at[:, cols], sc_out.at[:, cols], wr.at[1 + k])
        o.start()
        outs.append(o)

    for c in w_red:
        c.wait_recv()
    tot = ps_v[t].astype(F32)
    for i in range(n_t - 1):
        tot = tot + pr_v[i].astype(F32)
    kg_v[...] = tot[:, :head]
    vg_v[...] = tot[:, head:]
    kg_c = pltpu.make_async_copy(kg_v, kg_out, wr.at[1 + side])
    vg_c = pltpu.make_async_copy(vg_v, vg_out, wr.at[2 + side])
    kg_c.start()
    vg_c.start()

    for c in p1[:0]:
        c.wait_send()
    for c in g_sends:
        c.wait_send()
    for c in w_red:
        c.wait_send()

    @pl.when(pipe > 0)
    def _():
        for c in chain:
            c.wait_send()

    dq_c.wait()
    for o in outs:
        o.wait()
    kg_c.wait()
    vg_c.wait()


def per_device(sizes, section_input, norm_gain, key_weight, value_weight, queries, out_cotangent,
               segment_ids, upstream):
    n_pipe, n_dp, n_t = sizes
    seq, width = section_input.shape[3:]
    head = key_weight.shape[2]
    group = queries.shape[4] // head
    side = math.isqrt(n_dp)
    blk = width // n_dp
    quarter = seq // n_t
    two = 2 * head
    heads = group * head
    dims = (n_pipe, n_dp, n_t, side, seq, width, head, group)
    V = pltpu.VMEM
    DMA = pltpu.SemaphoreType.DMA
    any_spec = pl.BlockSpec(memory_space=pl.ANY)
    noff = n_dp - 1
    nz = n_t - 1
    na = 2 * (side - 1)
    sc, dq, kg, vg = pl.pallas_call(
        functools.partial(kernel, dims),
        out_shape=(
            jax.ShapeDtypeStruct((quarter, width), BF16),
            jax.ShapeDtypeStruct((seq, heads), BF16),
            jax.ShapeDtypeStruct((blk, head), F32),
            jax.ShapeDtypeStruct((blk, head), F32),
        ),
        in_specs=[any_spec] * 8,
        out_specs=(any_spec,) * 4,
        scratch_shapes=[
            V((seq, width), BF16),
            V((seq, width), BF16),
            V((width, two), BF16),
            V((blk, n_t * two), BF16),
            V((seq, heads), BF16),
            V((seq, heads), BF16),
            V((1, seq), jnp.int32),
            V((quarter, width), BF16),
            V((1, width), F32),
            V((quarter, 128), F32),
            V((n_dp, quarter, blk), BF16),
            V((seq, heads), BF16),
            V((seq, two), BF16),
            V((seq, 128), F32),
            V((n_t, quarter, 128), F32),
            V((side, side, quarter, n_t * two), BF16),
            V((side, side, quarter, blk), BF16),
            V((quarter, width), BF16),
            V((quarter, width), BF16),
            V((quarter, width), BF16),
            V((quarter, width), BF16),
            V((n_t, blk, two), BF16),
            V((nz, blk, two), BF16),
            V((blk, head), F32),
            V((blk, head), F32),
            DMA((19,)), DMA((3 + side,)),
            DMA((nz,)), DMA((nz,)),
            DMA((noff,)), DMA((noff,)),
            DMA((nz,)), DMA((nz,)),
            DMA((nz,)), DMA((nz,)),
            DMA((na,)), DMA((na,)),
            DMA((na,)), DMA((na,)),
            DMA((noff,)), DMA((noff,)),
            DMA((side,)), DMA((side,)),
            DMA((nz,)), DMA((nz,)),
        ],
        compiler_params=pltpu.CompilerParams(
            collective_id=0, has_side_effects=True, vmem_limit_bytes=62 << 20
        ),
        name="attention_backward",
    )(
        section_input.reshape(seq, width),
        norm_gain.reshape(1, width),
        key_weight.reshape(width, head),
        value_weight.reshape(width, head),
        queries.reshape(seq, heads),
        out_cotangent.reshape(seq, heads),
        segment_ids.reshape(1, seq),
        upstream.reshape(quarter, width),
    )
    return (
        sc.reshape(1, 1, 1, quarter, width),
        dq.reshape(1, 1, 1, seq, heads),
        kg[None],
        vg[None],
    )


def solution(mesh):
    sizes = tuple(mesh.shape[a] for a in ("pipe", "dp", "tensor"))
    return jax.shard_map(
        functools.partial(per_device, sizes),
        mesh=mesh,
        in_specs=(
            P("pipe", None, "dp", None, None),
            P("pipe", None),
            P("pipe", None, "tensor"),
            P("pipe", None, "tensor"),
            P("pipe", None, "dp", None, "tensor"),
            P("pipe", None, "dp", None, "tensor"),
            P(None, "dp", None),
            P(None, "dp", "tensor", None),
        ),
        out_specs=(
            P("pipe", None, "dp", "tensor", None),
            P("pipe", None, "dp", None, "tensor"),
            P("pipe", "dp", "tensor"),
            P("pipe", "dp", "tensor"),
        ),
        check_vma=False,
    )
```

time: 257 us -> 90.7 us (0.35)
  the two profiles are of different devices: /device:TPU:32 before, /device:TPU:64 now
where the time goes in v1:
time: 90.7 us; the launch traced here: 90.5 us
  Pallas kernels  83.9 us (93%)
  local copies, waits for them, and re-layouts  5.95 us (7%)
    pallas_call x1, Pallas kernels, per_device(): pl.pallas_call(functools.partial(kernel, dims), out_shape=(jax.ShapeDtype...  83.9 us
    unnamed x6, local copies, waits for them, and re-layouts  5.95 us

profile of v1, /device:TPU:64, one launch (start us, length us, event | category | flops | bytes accessed | tf_op | source)
XLA Modules:
  0.0 90.5 jit_solution(11900454437540385086)
XLA Ops:
  0.6 83.9 %attention_backward.1 = (bf16[32,8192]{1,0:T(8,128)(2,1)}, bf16[128,1024]{1,0:T(8,128)(2,1)}, f32[512,128]{1,0:T(8,128)}, f32[512,128]{1,0:T(8,128)}) custom-call(bf16[128,8192]{1,0:T(8,128)(2,1)} %bitcast.11, f32[1,8192]{1,0:T(1,128)} %gain_hbm.1, bf16[8192,128]{1,0:T(8,128)(2,1)} %bitcast.12, bf16[8192,128]{1,0:T(8,128)(2,1)} %bitcast.13, ...), custom_call_target="tpu_custom_call" | custom-call | tf_op jit(solution)/shard_map/attention_backward/pallas_call | solution.py:368
  84.6 0.0 copy-start
  84.6 1.9 %copy.16 = bf16[1,1,1,32,8192]{4,3,2,1,0:T(8,128)(2,1)} copy(bf16[1,1,1,32,8192]{4,3,2,1,0:T(8,128)(2,1)} %bitcast.14) | data formatting | bytes 1048576
  86.5 1.7 %copy.17 = bf16[1,1,1,128,1024]{4,3,2,1,0:T(8,128)(2,1)} copy(bf16[1,1,1,128,1024]{4,3,2,1,0:T(8,128)(2,1)} %bitcast.18) | data formatting | bytes 524288
  88.2 1.7 %copy.18 = f32[1,512,128]{2,1,0:T(8,128)} copy(f32[1,512,128]{2,1,0:T(8,128)} %bitcast.17) | data formatting | bytes 524288
  89.8 0.0 copy-done
  89.8 0.7 copy.19
Async XLA Ops:
  84.6 5.3 %copy-start = (f32[512,128]{1,0:T(8,128)S(1)}, f32[512,128]{1,0:T(8,128)}, u32[]{:S(2)}) copy-start(f32[512,128]{1,0:T(8,128)} %get-tuple-element.11) | copy-start | bytes 786436

commit v2 on v1

--- a/solution.py
+++ b/solution.py
@@ -12,6 +12,14 @@
 MESH = pl.DeviceIdType.MESH
 F32 = jnp.float32
 BF16 = jnp.bfloat16
+
+
+def far_first(side):
+    def hops(o):
+        return sum(min(a, side - a) for a in o)
+
+    every = [(dx, dy) for dy in range(side) for dx in range(side) if dx or dy]
+    return sorted(every, key=hops, reverse=True)
 
 
 def kernel(
@@ -51,7 +59,13 @@
             device_id=dev, device_id_type=MESH,
         )
 
-    offsets = [(dx, dy) for dy in range(side) for dx in range(side) if dx or dy]
+    def remote2(src, dst, ss, rs, dev):
+        return pltpu.make_async_remote_copy(
+            src_ref=src, dst_ref=dst, send_sem=ss, recv_sem=rs,
+            device_id=dev, device_id_type=MESH,
+        )
+
+    offsets = far_first(side)
 
     def dev_d(dd):
         return (pipe, dd, t)
@@ -116,12 +130,55 @@
     pl.semaphore_wait(barrier, len(offsets) + n_t - 1 + n_pipe - 1)
 
     own_rows = rows_of(0)
-    w_sends = []
-    for dt in range(1, n_t):
-        ref = wg_v.at[:, pl.ds(wcol, two)]
-        c = remote(ref, ref, ws_s, ws_r, dt - 1, dev_t(at_z(dt)))
-        c.start()
-        w_sends.append(c)
+    w_pieces = 4
+    prow = blk // w_pieces
+
+    def w_copy(lane, r, q, src, dev):
+        cols = pl.ds(pl.multiple_of(src * two, two), two)
+        ref = wg_v.at[pl.ds(q * prow, prow), cols]
+        return remote(ref, ref, ws_s, ws_r, (r * w_pieces + q) * 2 + lane, dev_t(dev))
+
+    def w_round(r):
+        for q in range(w_pieces):
+            @pl.when((t - r >= 0) & (t < n_t - 1))
+            def _():
+                w_copy(0, r, q, t - r, t + 1).start()
+
+            @pl.when((t + r < n_t) & (t > 0))
+            def _():
+                w_copy(1, r, q, t + r, t - 1).start()
+
+    def w_arrived(r, q):
+        @pl.when(t - r - 1 >= 0)
+        def _():
+            w_copy(0, r, q, t, t).wait_recv()
+
+        @pl.when(t + r + 1 < n_t)
+        def _():
+            w_copy(1, r, q, t, t).wait_recv()
+
+    def w_sent(r, q):
+        @pl.when((t - r >= 0) & (t < n_t - 1))
+        def _():
+            w_copy(0, r, q, t, t).wait_send()
+
+        @pl.when((t + r < n_t) & (t > 0))
+        def _():
+            w_copy(1, r, q, t, t).wait_send()
+
+    def w_forward(r):
+        for q in range(w_pieces):
+            w_arrived(r - 1, q)
+
+            @pl.when((t - r >= 0) & (t < n_t - 1))
+            def _():
+                w_copy(0, r, q, t - r, t + 1).start()
+
+            @pl.when((t + r < n_t) & (t > 0))
+            def _():
+                w_copy(1, r, q, t + r, t - 1).start()
+
+    w_round(0)
 
     def blk_cols(dd):
         return pl.ds(pl.multiple_of(dd * blk, blk), blk)
@@ -190,83 +247,117 @@
     ag_v[my, mx, :, pl.ds(wcol, two)] = dkv_v[own_rows, :]
     mr_v[0] = mp_v[own_rows, :]
 
+    w_forward(1)
+    for c in z_sends:
+        c.wait()
+
+    half = two * n_t // 2
+
+    def piece(h, yy, xx):
+        return ag_v.at[yy, xx, :, pl.ds(h * half, half)]
+
+    order = sorted(range(1, side), key=lambda i: -min(i, side - i))
+    na = side - 1
+    p1 = []
+    p2 = []
+    for i in order:
+        for h in range(2):
+            ref = piece(h, my, mx)
+            dd = at_xy(i, 0) if h == 0 else at_xy(0, i)
+            c = remote(ref, ref, a1_s, a1_r, h * na + i - 1, dev_d(dd))
+            c.start()
+            p1.append((i, h, c))
+
+    def spread(i, h):
+        yy = my if h == 0 else lax.rem(my + side - i, side)
+        xx = mx if h == 1 else lax.rem(mx + side - i, side)
+        ref = piece(h, yy, xx)
+        for j in order:
+            dd = at_xy(0, j) if h == 0 else at_xy(j, 0)
+            c = remote(ref, ref, a2_s, a2_r, (h * side + i) * na + j - 1, dev_d(dd))
+            c.start()
+            p2.append(c)
+
+    spread(0, 0)
+    spread(0, 1)
+
     dq = (jnp.dot(ds_, keys, preferred_element_type=F32) * factor).astype(BF16)
     for g in range(group):
         dq_v[:, g * head:(g + 1) * head] = dq[g * seq:(g + 1) * seq, :]
     dq_c = pltpu.make_async_copy(dq_v, dq_out, wr.at[0])
     dq_c.start()
 
-    for c in z_sends:
-        c.wait()
-
-    half = two * n_t // 2
-    p1 = []
-    for i in range(1, side):
-        ref = ag_v.at[my, mx, :, pl.ds(0, half)]
-        c = remote(ref, ref, a1_s, a1_r, i - 1, dev_d(at_xy(i, 0)))
-        c.start()
-        p1.append(c)
-    for i in range(1, side):
-        ref = ag_v.at[my, mx, :, pl.ds(half, half)]
-        c = remote(ref, ref, a1_s, a1_r, side - 1 + i - 1, dev_d(at_xy(0, i)))
-        c.start()
-        p1.append(c)
-    for c in p1[:side - 1]:
-        c.wait()
-    p2 = []
-    for i in range(1, side):
-        ref = ag_v.at[my, :, :, pl.ds(0, half)]
-        c = remote(ref, ref, a2_s, a2_r, i - 1, dev_d(at_xy(0, i)))
-        c.start()
-        p2.append(c)
-    for c in p1[side - 1:]:
-        c.wait()
-    for i in range(1, side):
-        ref = ag_v.at[:, mx, :, pl.ds(half, half)]
-        c = remote(ref, ref, a2_s, a2_r, side - 1 + i - 1, dev_d(at_xy(i, 0)))
-        c.start()
-        p2.append(c)
+    for i, h, c in p1:
+        c.wait_recv()
+        spread(i, h)
+    w_forward(2)
 
     for c in n_sends:
         c.wait()
-    for c in w_sends:
-        c.wait()
     nxt = nx_v[...].reshape(n_dp * quarter, blk).T
 
+    for i, h, c in p1:
+        c.wait_send()
     for c in p2:
         c.wait()
-
-    g_sends = []
-    gi = 0
-    for k in range(side):
-        yy = lax.rem(my + k, side)
-        lhs = ag_v[yy].reshape(side * quarter, n_t * two)
-        gk = lax.dot_general(lhs, wg_v[...], nt, preferred_element_type=F32).astype(BF16)
-        gs_v[yy] = gk.reshape(side, quarter, blk)
-        for dx in range(side):
-            if k == 0 and dx == 0:
-                continue
-            dd = at_xy(dx, k)
-            c = remote(
-                gs_v.at[yy, lax.rem(mx + dx, side)], gr_v.at[:, blk_cols(d)],
-                g_s, g_r, gi, dev_d(dd),
-            )
-            c.start()
-            g_sends.append(c)
-            gi += 1
-        if k == 0:
-            gr_v[:, blk_cols(d)] = gs_v[my, mx]
 
     full = ag_v[...].reshape(n_dp * quarter, n_t * two)
     part = jnp.dot(nxt, full, preferred_element_type=F32)
     for h in range(n_t):
         ps_v[h] = part[:, h * two:(h + 1) * two].astype(BF16)
-    w_red = []
-    for dt in range(1, n_t):
-        tt = at_z(dt)
-        c = remote(ps_v.at[tt], pr_v.at[dt - 1], p_s, p_r, dt - 1, dev_t(tt))
+
+    def p_copy(term, dev, slot):
+        return remote2(ps_v.at[term], pr_v.at[slot], p_s.at[term], p_r.at[slot], dev_t(dev))
+
+    last = n_t - 1
+
+    @pl.when(t == 0)
+    def _():
+        p_copy(3, 1, 1).start()
+        p_copy(2, 2, 0).start()
+        p_copy(1, 1, 0).start()
+        pr_v[3] = jnp.zeros(pr_v.shape[1:], BF16)
+
+    @pl.when(t == 1)
+    def _():
+        p_copy(2, 2, 1).start()
+        p_copy(0, 0, 1).start()
+
+    @pl.when(t == 2)
+    def _():
+        p_copy(1, 1, 2).start()
+        p_copy(3, 3, 2).start()
+
+    @pl.when(t == last)
+    def _():
+        p_copy(0, 2, 2).start()
+        p_copy(1, 1, 3).start()
+        p_copy(2, 2, 3).start()
+        pr_v[0] = jnp.zeros(pr_v.shape[1:], BF16)
+
+    for q in range(w_pieces):
+        w_arrived(2, q)
+    gfull = lax.dot_general(full, wg_v[...], nt, preferred_element_type=F32).astype(BF16)
+    gs_v[...] = gfull.reshape(n_dp, quarter, blk)
+    g_sends = []
+    for i, (dx, dy) in enumerate(offsets):
+        dd = at_xy(dx, dy)
+        c = remote(gs_v.at[dd], gr_v.at[i], g_s, g_r, i, dev_d(dd))
         c.start()
-        w_red.append(c)
+        g_sends.append(c)
+    gr_v[n_dp - 1] = gs_v[d]
+
+    @pl.when(t == 1)
+    def _():
+        p_copy(3, 1, 1).wait_recv()
+        ps_v[3] = (ps_v[3].astype(F32) + pr_v[1].astype(F32)).astype(BF16)
+        p_copy(3, 3, 1).start()
+
+    @pl.when(t == 2)
+    def _():
+        p_copy(0, 2, 2).wait_recv()
+        ps_v[0] = (ps_v[0].astype(F32) + pr_v[2].astype(F32)).astype(BF16)
+        p_copy(0, 0, 2).start()
 
     up_c.wait()
 
@@ -281,46 +372,46 @@
     inv = inv_v[:, :1]
     im = inv * inv * m
     prev = (lax.rem(pipe + n_pipe - 1, n_pipe), d, t)
-    cw = side * blk
     outs = []
     chain = []
-    gi = 0
+    per = n_dp // side
     for k in range(side):
-        yy = lax.rem(my + side - k, side)
-        cols = pl.ds(pl.multiple_of(yy * cw, cw), cw)
-        for dx in range(side):
-            if k == 0 and dx == 0:
-                continue
-            g_sends[gi].wait_recv()
-            gi += 1
-        c = remote(sb_v.at[:, cols], sr_v.at[:, cols], c_s, c_r, k, prev)
+        lo = k * per
+        c = remote(sb_v.at[pl.ds(lo, per)], sr_v.at[pl.ds(lo, per)], c_s, c_r, k, prev)
         chain.append(c)
+        for i in range(lo, lo + per):
+            if i < n_dp - 1:
+                g_sends[i].wait_recv()
 
         @pl.when(pipe < n_pipe - 1)
         def _():
             c.wait_recv()
 
-        for j in range(0, cw, step):
-            cc = pl.ds(pl.multiple_of(yy * cw + j, step), step)
-            gf = gr_v[:, cc].astype(F32)
+        for i in range(lo, lo + per):
+            dx, dy = offsets[i] if i < n_dp - 1 else (0, 0)
+            cc = blk_cols(at_xy(side - dx, side - dy))
+            gf = gr_v[i].astype(F32)
             xf = x_v[own_rows, cc].astype(F32)
-            con = inv * (gain_v[:, cc] * gf) - xf * im + sr_v[:, cc].astype(F32)
-            sb_v[:, cc] = con.astype(BF16)
+            con = inv * (gain_v[:, cc] * gf) - xf * im + sr_v[i].astype(F32)
+            sb_v[i] = con.astype(BF16)
             so_v[:, cc] = (up_v[:, cc].astype(F32) + con).astype(BF16)
 
         @pl.when(pipe > 0)
         def _():
             c.start()
 
-        o = pltpu.make_async_copy(so_v.at[:, cols], sc_out.at[:, cols], wr.at[1 + k])
-        o.start()
-        outs.append(o)
-
-    for c in w_red:
-        c.wait_recv()
+    o = pltpu.make_async_copy(so_v, sc_out, wr.at[1])
+    o.start()
+    outs.append(o)
+
+    for src in range(n_t):
+        @pl.when((t != src) & (abs(t - src) < last))
+        def _():
+            p_copy(0, 0, src).wait_recv()
+
     tot = ps_v[t].astype(F32)
-    for i in range(n_t - 1):
-        tot = tot + pr_v[i].astype(F32)
+    for i in range(1, n_t):
+        tot = tot + pr_v[at_z(i)].astype(F32)
     kg_v[...] = tot[:, :head]
     vg_v[...] = tot[:, head:]
     kg_c = pltpu.make_async_copy(kg_v, kg_out, wr.at[1 + side])
@@ -328,12 +419,15 @@
     kg_c.start()
     vg_c.start()
 
-    for c in p1[:0]:
-        c.wait_send()
     for c in g_sends:
         c.wait_send()
-    for c in w_red:
-        c.wait_send()
+    for r in range(n_t - 1):
+        for q in range(w_pieces):
+            w_sent(r, q)
+    for h in range(n_t):
+        @pl.when(t != h)
+        def _():
+            p_copy(h, 0, 0).wait_send()
 
     @pl.when(pipe > 0)
     def _():
@@ -345,6 +439,20 @@
         o.wait()
     kg_c.wait()
     vg_c.wait()
+
+
+def write_out(*refs):
+    n = 4
+    ins, outs, bufs, sems = refs[:n], refs[n:2 * n], refs[2 * n:3 * n], refs[3 * n]
+    loads = [pltpu.make_async_copy(ins[i], bufs[i], sems.at[0, i]) for i in range(n)]
+    stores = [pltpu.make_async_copy(bufs[i], outs[i], sems.at[1, i]) for i in range(n)]
+    for c in loads:
+        c.start()
+    for c, o in zip(loads, stores):
+        c.wait()
+        o.start()
+    for o in stores:
+        o.wait()
 
 
 def per_device(sizes, section_input, norm_gain, key_weight, value_weight, queries, out_cotangent,
@@ -392,25 +500,25 @@
             V((seq, 128), F32),
             V((n_t, quarter, 128), F32),
             V((side, side, quarter, n_t * two), BF16),
-            V((side, side, quarter, blk), BF16),
-            V((quarter, width), BF16),
-            V((quarter, width), BF16),
-            V((quarter, width), BF16),
+            V((n_dp, quarter, blk), BF16),
+            V((n_dp, quarter, blk), BF16),
+            V((n_dp, quarter, blk), BF16),
+            V((n_dp, quarter, blk), BF16),
             V((quarter, width), BF16),
             V((n_t, blk, two), BF16),
-            V((nz, blk, two), BF16),
+            V((n_t, blk, two), BF16),
             V((blk, head), F32),
             V((blk, head), F32),
             DMA((19,)), DMA((3 + side,)),
-            DMA((nz,)), DMA((nz,)),
+            DMA((8 * nz,)), DMA((8 * nz,)),
             DMA((noff,)), DMA((noff,)),
             DMA((nz,)), DMA((nz,)),
             DMA((nz,)), DMA((nz,)),
             DMA((na,)), DMA((na,)),
-            DMA((na,)), DMA((na,)),
+            DMA((side * na,)), DMA((side * na,)),
             DMA((noff,)), DMA((noff,)),
             DMA((side,)), DMA((side,)),
-            DMA((nz,)), DMA((nz,)),
+            DMA((n_t,)), DMA((n_t,)),
         ],
         compiler_params=pltpu.CompilerParams(
             collective_id=0, has_side_effects=True, vmem_limit_bytes=62 << 20
@@ -426,6 +534,16 @@
         segment_ids.reshape(1, seq),
         upstream.reshape(quarter, width),
     )
+    parts = (sc, dq, kg, vg)
+    sc, dq, kg, vg = pl.pallas_call(
+        write_out,
+        out_shape=tuple(jax.ShapeDtypeStruct(a.shape, a.dtype) for a in parts),
+        in_specs=[any_spec] * 4,
+        out_specs=(any_spec,) * 4,
+        scratch_shapes=[V(a.shape, a.dtype) for a in parts] + [DMA((2, 4))],
+        compiler_params=pltpu.CompilerParams(vmem_limit_bytes=62 << 20),
+        name="write_out",
+    )(*parts)
     return (
         sc.reshape(1, 1, 1, quarter, width),
         dq.reshape(1, 1, 1, seq, heads),

time: 90.7 us -> 64.2 us (0.71)
  the two profiles are of different devices: /device:TPU:64 before, /device:TPU:32 now
where the time goes in v2:
time: 64.2 us; the launch traced here: 64.1 us
  Pallas kernels  63.5 us (99%)
    pallas_call x1, Pallas kernels, per_device(): pl.pallas_call(functools.partial(kernel, dims), out_shape=(jax.ShapeDtype...  61.3 us
    pallas_call x1, Pallas kernels, per_device(): pl.pallas_call(write_out, out_shape=tuple((jax.ShapeDtypeStruct(a.shape,...  2.16 us

profile of v2, /device:TPU:32, one launch (start us, length us, event | category | flops | bytes accessed | tf_op | source)
XLA Modules:
  0.0 64.1 jit_solution(8214445319907626719)
XLA Ops:
  0.6 61.3 %attention_backward.1 = (bf16[32,8192]{1,0:T(8,128)(2,1)}, bf16[128,1024]{1,0:T(8,128)(2,1)}, f32[512,128]{1,0:T(8,128)}, f32[512,128]{1,0:T(8,128)}) custom-call(bf16[128,8192]{1,0:T(8,128)(2,1)} %bitcast.11, f32[1,8192]{1,0:T(1,128)} %gain_hbm.1, bf16[8192,128]{1,0:T(8,128)(2,1)} %bitcast.12, bf16[8192,128]{1,0:T(8,128)(2,1)} %bitcast.13, ...), custom_call_target="tpu_custom_call" | custom-call | tf_op jit(solution)/shard_map/attention_backward/pallas_call | solution.py:476
  62.0 2.2 %write_out.1 = (bf16[32,8192]{1,0:T(8,128)(2,1)}, bf16[128,1024]{1,0:T(8,128)(2,1)}, f32[512,128]{1,0:T(8,128)}, f32[512,128]{1,0:T(8,128)}) custom-call(bf16[32,8192]{1,0:T(8,128)(2,1)} %get-tuple-element.12.refs_0_, bf16[128,1024]{1,0:T(8,128)(2,1)} %get-tuple-element.13.refs_1_, f32[512,128]{1,0:T(8,128)} %get-tuple-element.14.refs_2_, ...), custom_call_target="tpu_custom_call" | custom-call | tf_op jit(solution)/shard_map/write_out/pallas_call | solution.py:538

commit v3 on v2

--- a/solution.py
+++ b/solution.py
@@ -27,8 +27,8 @@
     x_hbm, gain_hbm, kw_hbm, vw_hbm, q_hbm, oc_hbm, seg_hbm, up_hbm,
     sc_out, dq_out, kg_out, vg_out,
     x_v, n_v, w_v, wg_v, q_v, oc_v, seg_v, up_v, gain_v, inv_v,
-    nx_v, dq_v, dkv_v, mp_v, mr_v, ag_v, gs_v, gr_v, sr_v, sb_v, so_v,
-    ps_v, pr_v, kg_v, vg_v,
+    nx_v, dq_v, dkv_v, mp_v, mr_v, ag_v, ax_v, cf_v, fr_v, sr_v, sb_v, so_v,
+    pw_v, ps_v, pr_v, kg_v, vg_v,
     ld, wr, ws_s, ws_r, nx_s, nx_r, zk_s, zk_r, zm_s, zm_r,
     a1_s, a1_r, a2_s, a2_r, g_s, g_r, c_s, c_r, p_s, p_r,
 ):
@@ -59,12 +59,6 @@
             device_id=dev, device_id_type=MESH,
         )
 
-    def remote2(src, dst, ss, rs, dev):
-        return pltpu.make_async_remote_copy(
-            src_ref=src, dst_ref=dst, send_sem=ss, recv_sem=rs,
-            device_id=dev, device_id_type=MESH,
-        )
-
     offsets = far_first(side)
 
     def dev_d(dd):
@@ -78,10 +72,10 @@
         pl.semaphore_signal(barrier, inc=1, device_id=dev_d(at_xy(dx, dy)), device_id_type=MESH)
     for dt in range(1, n_t):
         pl.semaphore_signal(barrier, inc=1, device_id=dev_t(at_z(dt)), device_id_type=MESH)
-    for dp_ in range(1, n_pipe):
-        pl.semaphore_signal(
-            barrier, inc=1, device_id=(lax.rem(pipe + dp_, n_pipe), d, t), device_id_type=MESH
-        )
+
+    @pl.when(pipe < n_pipe - 1)
+    def _():
+        pl.semaphore_signal(barrier, inc=1, device_id=(pipe + 1, d, t), device_id_type=MESH)
 
     rows_d = pl.ds(pl.multiple_of(d * blk, blk), blk)
     wcol = pl.multiple_of(t * two, two)
@@ -89,10 +83,15 @@
     own_v = local(vw_hbm.at[rows_d], wg_v.at[:, pl.ds(wcol + head, head)], 1)
     gain_c = local(gain_hbm, gain_v, 2)
 
+    lo = lax.rem(t, 2)
+    hi = t // 2
+    partner = t + 1 - 2 * lo
+    order_q = (0, 2, 1, 3)
+
     def rows_of(i):
         return pl.ds(pl.multiple_of(lax.rem(t + i, n_t) * quarter, quarter), quarter)
 
-    x_cs = [local(x_hbm.at[rows_of(i)], x_v.at[rows_of(i)], 3 + i) for i in range(n_t)]
+    x_cs = {i: local(x_hbm.at[rows_of(i)], x_v.at[rows_of(i)], 3 + i) for i in order_q}
     n_w = 4
     wrows = width // n_w
     w_cs = []
@@ -119,15 +118,27 @@
         inv = lax.rsqrt(mean + NORM_EPS)
         for c in range(0, width, step):
             xf = x_v[r, c:c + step].astype(F32)
-            n_v[r, c:c + step] = (xf * inv * gain_v[:, c:c + step]).astype(BF16)
+            normed = (xf * inv * gain_v[:, c:c + step]).astype(BF16)
+            qi = lax.rem(t + i, n_t)
+            n_v[qi // 2, lax.rem(qi, 2), :, c:c + step] = normed
         return inv
 
     gain_c.wait()
     x_cs[0].wait()
     inv_v[...] = jnp.broadcast_to(norm_quarter(0), (quarter, 128))
+    x_cs[2].wait()
+    norm_quarter(2)
     own_k.wait()
     own_v.wait()
-    pl.semaphore_wait(barrier, len(offsets) + n_t - 1 + n_pipe - 1)
+    peers = len(offsets) + n_t - 1
+
+    @pl.when(pipe > 0)
+    def _():
+        pl.semaphore_wait(barrier, peers + 1)
+
+    @pl.when(pipe == 0)
+    def _():
+        pl.semaphore_wait(barrier, peers)
 
     own_rows = rows_of(0)
     w_pieces = 4
@@ -183,15 +194,33 @@
     def blk_cols(dd):
         return pl.ds(pl.multiple_of(dd * blk, blk), blk)
 
+    nw = blk // 2
+
+    def part_cols(dd, p):
+        return pl.ds(pl.multiple_of(dd * blk + p * nw, nw), nw)
+
+    oth = 1 - hi
     n_sends = []
     for i, (dx, dy) in enumerate(offsets):
         dd = at_xy(dx, dy)
-        c = remote(n_v.at[own_rows, blk_cols(dd)], nx_v.at[d], nx_s, nx_r, i, dev_d(dd))
+        c = remote(n_v.at[hi, lo, :, blk_cols(dd)], nx_v.at[my, mx, hi], nx_s, nx_r, i, dev_d(dd))
         c.start()
         n_sends.append(c)
-    nx_v[d] = n_v[own_rows, blk_cols(d)]
-
-    for i in range(1, n_t):
+    nx_v[my, mx] = n_v[:, lo, :, blk_cols(d)]
+
+    def send_other(p):
+        for i, (dx, dy) in enumerate(offsets):
+            dd = at_xy(dx, dy)
+            c = remote(
+                n_v.at[oth, lo, :, part_cols(dd, p)], nx_v.at[my, mx, oth, :, pl.ds(p * nw, nw)],
+                nx_s, nx_r, (p + 1) * len(offsets) + i, dev_d(dd),
+            )
+            c.start()
+            n_sends.append(c)
+
+    send_other(0)
+
+    for i in (1, 3):
         x_cs[i].wait()
         norm_quarter(i)
 
@@ -200,7 +229,7 @@
         w_cs[2 * i].wait()
         w_cs[2 * i + 1].wait()
         kv = kv + jnp.dot(
-            n_v[:, i * wrows:(i + 1) * wrows], w_v[i * wrows:(i + 1) * wrows, :],
+            n_v[:, :, :, i * wrows:(i + 1) * wrows].reshape(seq, wrows), w_v[i * wrows:(i + 1) * wrows, :],
             preferred_element_type=F32,
         )
     keys = kv[:, :head].astype(BF16)
@@ -233,53 +262,105 @@
     msum = jnp.sum(
         dk.astype(F32) * kv[:, :head] + dv.astype(F32) * kv[:, head:], axis=-1, keepdims=True
     )
-    mp_v[...] = jnp.broadcast_to(msum, (seq, 128))
+    mfull = jnp.broadcast_to(msum, (seq, 128))
+    mtop = mfull.astype(BF16)
+    mlow = (mfull - mtop.astype(F32)).astype(BF16)
+    lane = lax.broadcasted_iota(jnp.int32, (seq, 128), 1)
+    mp_v[...] = jnp.where(lane < 64, mtop.astype(F32), mlow.astype(F32)).astype(BF16)
+
+    def head_cols(h):
+        return pl.ds(pl.multiple_of(h * two + (h // 2) * 128, 128), two)
+
+    def extra_cols(par):
+        return pl.ds(pl.multiple_of(par * two, two), two)
 
     z_sends = []
     for dt in range(1, n_t):
         tt = at_z(dt)
         r = pl.ds(pl.multiple_of(tt * quarter, quarter), quarter)
-        c1 = remote(dkv_v.at[r], ag_v.at[my, mx, :, pl.ds(wcol, two)], zk_s, zk_r, dt - 1, dev_t(tt))
-        c1.start()
-        c2 = remote(mp_v.at[r], mr_v.at[dt], zm_s, zm_r, dt - 1, dev_t(tt))
-        c2.start()
-        z_sends += [c1, c2]
-    ag_v[my, mx, :, pl.ds(wcol, two)] = dkv_v[own_rows, :]
+        c = remote(dkv_v.at[r], ag_v.at[my, mx, :, head_cols(t)], zk_s, zk_r, dt - 1, dev_t(tt))
+        c.start()
+        z_sends.append(c)
+    r = pl.ds(pl.multiple_of(lax.rem(partner + 2, n_t) * quarter, quarter), quarter)
+    c = remote(dkv_v.at[r], ax_v.at[my, mx, :, extra_cols(lo)], zk_s, zk_r, n_t - 1, dev_t(partner))
+    c.start()
+    z_sends.append(c)
+    m_sends = []
+    for dt in range(1, n_t):
+        tt = at_z(dt)
+        r = pl.ds(pl.multiple_of(tt * quarter, quarter), quarter)
+        c = remote(mp_v.at[r], mr_v.at[dt], zm_s, zm_r, dt - 1, dev_t(tt))
+        c.start()
+        m_sends.append(c)
+    ag_v[my, mx, :, head_cols(t)] = dkv_v[own_rows, :]
+    ax_v[my, mx, :, extra_cols(lo)] = dkv_v[rows_of(2), :]
     mr_v[0] = mp_v[own_rows, :]
 
-    w_forward(1)
     for c in z_sends:
         c.wait()
-
-    half = two * n_t // 2
-
-    def piece(h, yy, xx):
-        return ag_v.at[yy, xx, :, pl.ds(h * half, half)]
+    for c in m_sends:
+        c.wait()
+
+    m = mr_v[0].astype(F32)
+    for h in range(1, n_t):
+        m = m + mr_v[h].astype(F32)
+    m = (m[:, :1] + m[:, 64:65]) * (1.0 / width)
+    lane = lax.broadcasted_iota(jnp.int32, (quarter, 128), 1)
+    inv_f = inv_v[...]
+    both = jnp.where(lane < 64, inv_f, inv_f * m)
+    top = both.astype(BF16).astype(F32)
+    fine = lax.rem(lane, 64) >= 32
+    ag_v[my, mx, :, 2 * two:2 * two + 128] = jnp.where(fine, both - top, top).astype(BF16)
 
     order = sorted(range(1, side), key=lambda i: -min(i, side - i))
     na = side - 1
-    p1 = []
-    p2 = []
-    for i in order:
-        for h in range(2):
-            ref = piece(h, my, mx)
-            dd = at_xy(i, 0) if h == 0 else at_xy(0, i)
-            c = remote(ref, ref, a1_s, a1_r, h * na + i - 1, dev_d(dd))
+
+    class Gather:
+        def __init__(self, buf, ss, rs, cuts):
+            self.buf, self.ss, self.rs, self.cuts = buf, ss, rs, cuts
+            self.first, self.second = [], []
+
+        def piece(self, h, yy, xx):
+            return self.buf.at[yy, xx, :, pl.ds(*self.cuts[h])]
+
+        def send(self, ref, i, h, axis, dst):
+            dd = at_xy(i, 0) if axis == 0 else at_xy(0, i)
+            c = remote(ref, ref, self.ss, self.rs, dst, dev_d(dd))
             c.start()
-            p1.append((i, h, c))
-
-    def spread(i, h):
-        yy = my if h == 0 else lax.rem(my + side - i, side)
-        xx = mx if h == 1 else lax.rem(mx + side - i, side)
-        ref = piece(h, yy, xx)
-        for j in order:
-            dd = at_xy(0, j) if h == 0 else at_xy(j, 0)
-            c = remote(ref, ref, a2_s, a2_r, (h * side + i) * na + j - 1, dev_d(dd))
-            c.start()
-            p2.append(c)
-
-    spread(0, 0)
-    spread(0, 1)
+            return c
+
+        def begin(self):
+            for i in order:
+                for h in range(2):
+                    ref = self.piece(h, my, mx)
+                    self.first.append((i, h, self.send(ref, i, h, h, h * na + i - 1)))
+            self.spread(0, 0)
+            self.spread(0, 1)
+
+        def spread(self, i, h):
+            yy = my if h == 0 else lax.rem(my + side - i, side)
+            xx = mx if h == 1 else lax.rem(mx + side - i, side)
+            ref = self.piece(h, yy, xx)
+            for j in order:
+                n = 2 * na + (h * side + i) * na + j - 1
+                self.second.append(self.send(ref, j, h, 1 - h, n))
+
+        def forward(self):
+            for i, h, c in self.first:
+                c.wait_recv()
+                self.spread(i, h)
+
+        def finish(self):
+            for i, h, c in self.first:
+                c.wait_send()
+            for c in self.second:
+                c.wait()
+
+    cut = 2 * two + 128
+    main = Gather(ag_v, a1_s, a1_r, ((0, cut), (cut, 2 * two)))
+    extra = Gather(ax_v, a2_s, a2_r, ((0, two), (two, two)))
+    main.begin()
+    w_forward(1)
 
     dq = (jnp.dot(ds_, keys, preferred_element_type=F32) * factor).astype(BF16)
     for g in range(group):
@@ -287,131 +368,111 @@
     dq_c = pltpu.make_async_copy(dq_v, dq_out, wr.at[0])
     dq_c.start()
 
-    for i, h, c in p1:
-        c.wait_recv()
-        spread(i, h)
+    main.forward()
     w_forward(2)
-
-    for c in n_sends:
+    for c in n_sends[:len(offsets)]:
         c.wait()
-    nxt = nx_v[...].reshape(n_dp * quarter, blk).T
-
-    for i, h, c in p1:
-        c.wait_send()
-    for c in p2:
-        c.wait()
-
-    full = ag_v[...].reshape(n_dp * quarter, n_t * two)
-    part = jnp.dot(nxt, full, preferred_element_type=F32)
-    for h in range(n_t):
-        ps_v[h] = part[:, h * two:(h + 1) * two].astype(BF16)
-
-    def p_copy(term, dev, slot):
-        return remote2(ps_v.at[term], pr_v.at[slot], p_s.at[term], p_r.at[slot], dev_t(dev))
-
-    last = n_t - 1
-
-    @pl.when(t == 0)
-    def _():
-        p_copy(3, 1, 1).start()
-        p_copy(2, 2, 0).start()
-        p_copy(1, 1, 0).start()
-        pr_v[3] = jnp.zeros(pr_v.shape[1:], BF16)
-
-    @pl.when(t == 1)
-    def _():
-        p_copy(2, 2, 1).start()
-        p_copy(0, 0, 1).start()
-
-    @pl.when(t == 2)
-    def _():
-        p_copy(1, 1, 2).start()
-        p_copy(3, 3, 2).start()
-
-    @pl.when(t == last)
-    def _():
-        p_copy(0, 2, 2).start()
-        p_copy(1, 1, 3).start()
-        p_copy(2, 2, 3).start()
-        pr_v[0] = jnp.zeros(pr_v.shape[1:], BF16)
+    main.finish()
+    extra.begin()
+    send_other(1)
 
     for q in range(w_pieces):
         w_arrived(2, q)
-    gfull = lax.dot_general(full, wg_v[...], nt, preferred_element_type=F32).astype(BF16)
-    gs_v[...] = gfull.reshape(n_dp, quarter, blk)
-    g_sends = []
-    for i, (dx, dy) in enumerate(offsets):
-        dd = at_xy(dx, dy)
-        c = remote(gs_v.at[dd], gr_v.at[i], g_s, g_r, i, dev_d(dd))
-        c.start()
-        g_sends.append(c)
-    gr_v[n_dp - 1] = gs_v[d]
-
-    @pl.when(t == 1)
+    tokens = n_dp * quarter
+    row = side * quarter
+    gain_b = gain_v[:, blk_cols(d)]
+    gain_r = 1.0 / gain_b
+    prev = (lax.rem(pipe + n_pipe - 1, n_pipe), d, t)
+    dys = (2, 1, 3, 0)
+
+    def chain_copy(j):
+        return remote(sb_v.at[j], sr_v.at[j], c_s, c_r, j, prev)
+
+    def deliver(j):
+        dy = dys[j]
+        for dx in range(side):
+            i = j * side + dx
+            if dx or dy:
+                deliver_copy(i).start()
+            else:
+                fr_v[i] = sb_v[j, mx]
+
+    def deliver_copy(i):
+        dx, dy = i % side, dys[i // side]
+        src = sb_v.at[i // side, lax.rem(mx + dx, side)]
+        return remote(src, fr_v.at[i], g_s, g_r, i, dev_d(at_xy(dx, dy)))
+
+    for j, dy in enumerate(dys):
+        yy = lax.rem(my + dy, side)
+        lhs = ag_v[yy, :, :, :2 * two].reshape(row, 2 * two)
+        g = lax.dot_general(lhs, wg_v[:, :2 * two], nt, preferred_element_type=F32)
+        lhs = ag_v[yy, :, :, cut:].reshape(row, 2 * two)
+        g = g + lax.dot_general(lhs, wg_v[:, 2 * two:], nt, preferred_element_type=F32)
+        sc = ag_v[yy, :, :, 2 * two:cut].reshape(row, 128).astype(F32)
+        alpha = sc[:, :1] + sc[:, 32:33]
+        beta = sc[:, 64:65] + sc[:, 96:97]
+        nrm = nx_v[yy, :, hi].reshape(row, blk).astype(F32)
+        con = alpha * (gain_b * g) - (beta * nrm) * gain_r
+        cf_v[j] = con
+
+        @pl.when(pipe == n_pipe - 1)
+        def _():
+            sb_v[j] = con.astype(BF16).reshape(side, quarter, blk)
+            chain_copy(j).start()
+            deliver(j)
+
+    def chain():
+        for j in range(side):
+            chain_copy(j).wait_recv()
+            tot = cf_v[j] + sr_v[j].reshape(row, blk).astype(F32)
+            sb_v[j] = tot.astype(BF16).reshape(side, quarter, blk)
+
+            @pl.when(pipe > 0)
+            def _():
+                chain_copy(j).start()
+
+            deliver(j)
+
+    @pl.when(pipe == n_pipe - 2)
     def _():
-        p_copy(3, 1, 1).wait_recv()
-        ps_v[3] = (ps_v[3].astype(F32) + pr_v[1].astype(F32)).astype(BF16)
-        p_copy(3, 3, 1).start()
-
-    @pl.when(t == 2)
+        chain()
+
+    extra.forward()
+
+    for c in n_sends[len(offsets):]:
+        c.wait()
+    extra.finish()
+    nxt_own = nx_v[:, :, hi].reshape(tokens, blk).T
+    nxt_oth = nx_v[:, :, oth].reshape(tokens, blk).T
+    pair_at = pl.multiple_of(hi * (2 * two + 128), 128)
+    own_pair = ag_v[:, :, :, pl.ds(pair_at, 2 * two)]
+    part = jnp.dot(nxt_own, own_pair.reshape(tokens, 2 * two), preferred_element_type=F32)
+    part = part + jnp.dot(
+        nxt_oth, ax_v[...].reshape(tokens, 2 * two), preferred_element_type=F32
+    )
+    for h in range(2):
+        pw_v[h] = part[:, h * two:(h + 1) * two]
+    ps_v[...] = pw_v[1 - lo].astype(BF16)
+    p_c = remote(ps_v, pr_v, p_s, p_r, 0, dev_t(partner))
+    p_c.start()
+
+    @pl.when(pipe < n_pipe - 2)
     def _():
-        p_copy(0, 2, 2).wait_recv()
-        ps_v[0] = (ps_v[0].astype(F32) + pr_v[2].astype(F32)).astype(BF16)
-        p_copy(0, 0, 2).start()
+        chain()
 
     up_c.wait()
-
-    @pl.when(pipe == n_pipe - 1)
-    def _():
-        sr_v[...] = jnp.zeros(sr_v.shape, BF16)
-
-    m = mr_v[0]
-    for h in range(1, n_t):
-        m = m + mr_v[h]
-    m = m[:, :1] * (1.0 / width)
-    inv = inv_v[:, :1]
-    im = inv * inv * m
-    prev = (lax.rem(pipe + n_pipe - 1, n_pipe), d, t)
-    outs = []
-    chain = []
-    per = n_dp // side
-    for k in range(side):
-        lo = k * per
-        c = remote(sb_v.at[pl.ds(lo, per)], sr_v.at[pl.ds(lo, per)], c_s, c_r, k, prev)
-        chain.append(c)
-        for i in range(lo, lo + per):
-            if i < n_dp - 1:
-                g_sends[i].wait_recv()
-
-        @pl.when(pipe < n_pipe - 1)
-        def _():
-            c.wait_recv()
-
-        for i in range(lo, lo + per):
-            dx, dy = offsets[i] if i < n_dp - 1 else (0, 0)
-            cc = blk_cols(at_xy(side - dx, side - dy))
-            gf = gr_v[i].astype(F32)
-            xf = x_v[own_rows, cc].astype(F32)
-            con = inv * (gain_v[:, cc] * gf) - xf * im + sr_v[i].astype(F32)
-            sb_v[i] = con.astype(BF16)
-            so_v[:, cc] = (up_v[:, cc].astype(F32) + con).astype(BF16)
-
-        @pl.when(pipe > 0)
-        def _():
-            c.start()
-
+    for i in range(n_dp):
+        dx, dy = i % side, dys[i // side]
+        if dx or dy:
+            deliver_copy(i).wait_recv()
+        cc = blk_cols(at_xy(side - dx, side - dy))
+        so_v[:, cc] = (up_v[:, cc].astype(F32) + fr_v[i].astype(F32)).astype(BF16)
     o = pltpu.make_async_copy(so_v, sc_out, wr.at[1])
     o.start()
-    outs.append(o)
-
-    for src in range(n_t):
-        @pl.when((t != src) & (abs(t - src) < last))
-        def _():
-            p_copy(0, 0, src).wait_recv()
-
-    tot = ps_v[t].astype(F32)
-    for i in range(1, n_t):
-        tot = tot + pr_v[at_z(i)].astype(F32)
+    outs = [o]
+
+    p_c.wait()
+    tot = pw_v[lo] + pr_v[...].astype(F32)
     kg_v[...] = tot[:, :head]
     vg_v[...] = tot[:, head:]
     kg_c = pltpu.make_async_copy(kg_v, kg_out, wr.at[1 + side])
@@ -419,20 +480,17 @@
     kg_c.start()
     vg_c.start()
 
-    for c in g_sends:
-        c.wait_send()
+    for i in range(n_dp):
+        if i % side or dys[i // side]:
+            deliver_copy(i).wait_send()
     for r in range(n_t - 1):
         for q in range(w_pieces):
             w_sent(r, q)
-    for h in range(n_t):
-        @pl.when(t != h)
-        def _():
-            p_copy(h, 0, 0).wait_send()
 
     @pl.when(pipe > 0)
     def _():
-        for c in chain:
-            c.wait_send()
+        for k in range(4):
+            chain_copy(k).wait_send()
 
     dq_c.wait()
     for o in outs:
@@ -485,7 +543,7 @@
         out_specs=(any_spec,) * 4,
         scratch_shapes=[
             V((seq, width), BF16),
-            V((seq, width), BF16),
+            V((2, 2, quarter, width), BF16),
             V((width, two), BF16),
             V((blk, n_t * two), BF16),
             V((seq, heads), BF16),
@@ -494,31 +552,33 @@
             V((quarter, width), BF16),
             V((1, width), F32),
             V((quarter, 128), F32),
-            V((n_dp, quarter, blk), BF16),
+            V((side, side, 2, quarter, blk), BF16),
             V((seq, heads), BF16),
             V((seq, two), BF16),
-            V((seq, 128), F32),
-            V((n_t, quarter, 128), F32),
-            V((side, side, quarter, n_t * two), BF16),
+            V((seq, 128), BF16),
+            V((n_t, quarter, 128), BF16),
+            V((side, side, quarter, n_t * two + 128), BF16),
+            V((side, side, quarter, 2 * two), BF16),
+            V((side, side * quarter, blk), F32),
             V((n_dp, quarter, blk), BF16),
-            V((n_dp, quarter, blk), BF16),
-            V((n_dp, quarter, blk), BF16),
-            V((n_dp, quarter, blk), BF16),
+            V((side, side, quarter, blk), BF16),
+            V((side, side, quarter, blk), BF16),
             V((quarter, width), BF16),
-            V((n_t, blk, two), BF16),
-            V((n_t, blk, two), BF16),
+            V((2, blk, two), F32),
+            V((blk, two), BF16),
+            V((blk, two), BF16),
             V((blk, head), F32),
             V((blk, head), F32),
             DMA((19,)), DMA((3 + side,)),
             DMA((8 * nz,)), DMA((8 * nz,)),
-            DMA((noff,)), DMA((noff,)),
+            DMA((3 * noff,)), DMA((3 * noff,)),
+            DMA((n_t,)), DMA((n_t,)),
             DMA((nz,)), DMA((nz,)),
-            DMA((nz,)), DMA((nz,)),
-            DMA((na,)), DMA((na,)),
-            DMA((side * na,)), DMA((side * na,)),
-            DMA((noff,)), DMA((noff,)),
-            DMA((side,)), DMA((side,)),
-            DMA((n_t,)), DMA((n_t,)),
+            DMA((na + side * na,)), DMA((na + side * na,)),
+            DMA((na + side * na,)), DMA((na + side * na,)),
+            DMA((n_dp,)), DMA((n_dp,)),
+            DMA((4,)), DMA((4,)),
+            DMA((1,)), DMA((1,)),
         ],
         compiler_params=pltpu.CompilerParams(
             collective_id=0, has_side_effects=True, vmem_limit_bytes=62 << 20

time: 64.2 us -> 60.2 us (0.938)
  Pallas kernels: 63.5 us -> 59.4 us
    pallas_call x1, Pallas kernels: 61.3 us -> 57.3 us  [per_device(): pl.pallas_call(functools.partial(kernel, dims), out_shape=(jax.ShapeDtype...]
where the time goes in v3:
time: 60.2 us; the launch traced here: 60.1 us
  Pallas kernels  59.4 us (99%)
  between operations  0.64 us (1%)
    pallas_call x1, Pallas kernels, per_device(): pl.pallas_call(functools.partial(kernel, dims), out_shape=(jax.ShapeDtype...  57.3 us
    pallas_call x1, Pallas kernels, per_device(): pl.pallas_call(write_out, out_shape=tuple((jax.ShapeDtypeStruct(a.shape,...  2.16 us

profile of v3, /device:TPU:32, one launch (start us, length us, event | category | flops | bytes accessed | tf_op | source)
XLA Modules:
  0.0 60.1 jit_solution(11475217280101228983)
XLA Ops:
  0.6 57.3 %attention_backward.1 = (bf16[32,8192]{1,0:T(8,128)(2,1)}, bf16[128,1024]{1,0:T(8,128)(2,1)}, f32[512,128]{1,0:T(8,128)}, f32[512,128]{1,0:T(8,128)}) custom-call(bf16[128,8192]{1,0:T(8,128)(2,1)} %bitcast.11, f32[1,8192]{1,0:T(1,128)} %gain_hbm.1, bf16[8192,128]{1,0:T(8,128)(2,1)} %bitcast.12, bf16[8192,128]{1,0:T(8,128)(2,1)} %bitcast.13, ...), custom_call_target="tpu_custom_call" | custom-call | tf_op jit(solution)/shard_map/attention_backward/pallas_call | solution.py:534
  57.9 2.2 %write_out.1 = (bf16[32,8192]{1,0:T(8,128)(2,1)}, bf16[128,1024]{1,0:T(8,128)(2,1)}, f32[512,128]{1,0:T(8,128)}, f32[512,128]{1,0:T(8,128)}) custom-call(bf16[32,8192]{1,0:T(8,128)(2,1)} %get-tuple-element.12.refs_0_, bf16[128,1024]{1,0:T(8,128)(2,1)} %get-tuple-element.13.refs_1_, f32[512,128]{1,0:T(8,128)} %get-tuple-element.14.refs_2_, ...), custom_call_target="tpu_custom_call" | custom-call | tf_op jit(solution)/shard_map/write_out/pallas_call | solution.py:598

commit v4 on v3

--- a/solution.py
+++ b/solution.py
@@ -27,9 +27,9 @@
     x_hbm, gain_hbm, kw_hbm, vw_hbm, q_hbm, oc_hbm, seg_hbm, up_hbm,
     sc_out, dq_out, kg_out, vg_out,
     x_v, n_v, w_v, wg_v, q_v, oc_v, seg_v, up_v, gain_v, inv_v,
-    nx_v, dq_v, dkv_v, mp_v, mr_v, ag_v, ax_v, cf_v, fr_v, sr_v, sb_v, so_v,
-    pw_v, ps_v, pr_v, kg_v, vg_v,
-    ld, wr, ws_s, ws_r, nx_s, nx_r, zk_s, zk_r, zm_s, zm_r,
+    nx_v, dkv_v, mp_v, mr_v, ag_v, ax_v, cf_v, fr_v, sr_v, sb_v,
+    pw_v, ps_v, pr_v,
+    ld, ws_s, ws_r, nx_s, nx_r, zk_s, zk_r, zm_s, zm_r,
     a1_s, a1_r, a2_s, a2_r, g_s, g_r, c_s, c_r, p_s, p_r,
 ):
     n_pipe, n_dp, n_t, side, seq, width, head, group = dims
@@ -123,73 +123,74 @@
             n_v[qi // 2, lax.rem(qi, 2), :, c:c + step] = normed
         return inv
 
+    own_k.wait()
+    own_v.wait()
+    peers = len(offsets) + n_t - 1
+
+    @pl.when(pipe > 0)
+    def _():
+        pl.semaphore_wait(barrier, peers + 1)
+
+    @pl.when(pipe == 0)
+    def _():
+        pl.semaphore_wait(barrier, peers)
+
+    own_rows = rows_of(0)
+    w_pieces = 4
+    prow = blk // w_pieces
+
+    def w_copy(lane, r, q, src, dev):
+        cols = pl.ds(pl.multiple_of(src * two, two), two)
+        ref = wg_v.at[pl.ds(q * prow, prow), cols]
+        return remote(ref, ref, ws_s, ws_r, (r * w_pieces + q) * 2 + lane, dev_t(dev))
+
+    def w_round(r):
+        for q in range(w_pieces):
+            @pl.when((t - r >= 0) & (t < n_t - 1))
+            def _():
+                w_copy(0, r, q, t - r, t + 1).start()
+
+            @pl.when((t + r < n_t) & (t > 0))
+            def _():
+                w_copy(1, r, q, t + r, t - 1).start()
+
+    def w_arrived(r, q):
+        @pl.when(t - r - 1 >= 0)
+        def _():
+            w_copy(0, r, q, t, t).wait_recv()
+
+        @pl.when(t + r + 1 < n_t)
+        def _():
+            w_copy(1, r, q, t, t).wait_recv()
+
+    def w_sent(r, q):
+        @pl.when((t - r >= 0) & (t < n_t - 1))
+        def _():
+            w_copy(0, r, q, t, t).wait_send()
+
+        @pl.when((t + r < n_t) & (t > 0))
+        def _():
+            w_copy(1, r, q, t, t).wait_send()
+
+    def w_forward(r):
+        for q in range(w_pieces):
+            w_arrived(r - 1, q)
+
+            @pl.when((t - r >= 0) & (t < n_t - 1))
+            def _():
+                w_copy(0, r, q, t - r, t + 1).start()
+
+            @pl.when((t + r < n_t) & (t > 0))
+            def _():
+                w_copy(1, r, q, t + r, t - 1).start()
+
+    w_round(0)
+
     gain_c.wait()
     x_cs[0].wait()
     inv_v[...] = jnp.broadcast_to(norm_quarter(0), (quarter, 128))
     x_cs[2].wait()
     norm_quarter(2)
-    own_k.wait()
-    own_v.wait()
-    peers = len(offsets) + n_t - 1
-
-    @pl.when(pipe > 0)
-    def _():
-        pl.semaphore_wait(barrier, peers + 1)
-
-    @pl.when(pipe == 0)
-    def _():
-        pl.semaphore_wait(barrier, peers)
-
-    own_rows = rows_of(0)
-    w_pieces = 4
-    prow = blk // w_pieces
-
-    def w_copy(lane, r, q, src, dev):
-        cols = pl.ds(pl.multiple_of(src * two, two), two)
-        ref = wg_v.at[pl.ds(q * prow, prow), cols]
-        return remote(ref, ref, ws_s, ws_r, (r * w_pieces + q) * 2 + lane, dev_t(dev))
-
-    def w_round(r):
-        for q in range(w_pieces):
-            @pl.when((t - r >= 0) & (t < n_t - 1))
-            def _():
-                w_copy(0, r, q, t - r, t + 1).start()
-
-            @pl.when((t + r < n_t) & (t > 0))
-            def _():
-                w_copy(1, r, q, t + r, t - 1).start()
-
-    def w_arrived(r, q):
-        @pl.when(t - r - 1 >= 0)
-        def _():
-            w_copy(0, r, q, t, t).wait_recv()
-
-        @pl.when(t + r + 1 < n_t)
-        def _():
-            w_copy(1, r, q, t, t).wait_recv()
-
-    def w_sent(r, q):
-        @pl.when((t - r >= 0) & (t < n_t - 1))
-        def _():
-            w_copy(0, r, q, t, t).wait_send()
-
-        @pl.when((t + r < n_t) & (t > 0))
-        def _():
-            w_copy(1, r, q, t, t).wait_send()
-
-    def w_forward(r):
-        for q in range(w_pieces):
-            w_arrived(r - 1, q)
-
-            @pl.when((t - r >= 0) & (t < n_t - 1))
-            def _():
-                w_copy(0, r, q, t - r, t + 1).start()
-
-            @pl.when((t + r < n_t) & (t > 0))
-            def _():
-                w_copy(1, r, q, t + r, t - 1).start()
-
-    w_round(0)
 
     def blk_cols(dd):
         return pl.ds(pl.multiple_of(dd * blk, blk), blk)
@@ -208,15 +209,17 @@
         n_sends.append(c)
     nx_v[my, mx] = n_v[:, lo, :, blk_cols(d)]
 
-    def send_other(p):
+    def others(p):
         for i, (dx, dy) in enumerate(offsets):
             dd = at_xy(dx, dy)
-            c = remote(
+            yield remote(
                 n_v.at[oth, lo, :, part_cols(dd, p)], nx_v.at[my, mx, oth, :, pl.ds(p * nw, nw)],
                 nx_s, nx_r, (p + 1) * len(offsets) + i, dev_d(dd),
             )
+
+    def send_other(p):
+        for c in others(p):
             c.start()
-            n_sends.append(c)
 
     send_other(0)
 
@@ -318,43 +321,48 @@
     class Gather:
         def __init__(self, buf, ss, rs, cuts):
             self.buf, self.ss, self.rs, self.cuts = buf, ss, rs, cuts
-            self.first, self.second = [], []
 
         def piece(self, h, yy, xx):
             return self.buf.at[yy, xx, :, pl.ds(*self.cuts[h])]
 
-        def send(self, ref, i, h, axis, dst):
+        def copy(self, ref, i, axis, n):
             dd = at_xy(i, 0) if axis == 0 else at_xy(0, i)
-            c = remote(ref, ref, self.ss, self.rs, dst, dev_d(dd))
-            c.start()
-            return c
+            return remote(ref, ref, self.ss, self.rs, n, dev_d(dd))
+
+        def first(self, i, h):
+            return self.copy(self.piece(h, my, mx), i, h, h * na + i - 1)
+
+        def second(self, i, h, j):
+            yy = my if h == 0 else lax.rem(my + side - i, side)
+            xx = mx if h == 1 else lax.rem(mx + side - i, side)
+            n = 2 * na + (h * side + i) * na + j - 1
+            return self.copy(self.piece(h, yy, xx), j, 1 - h, n)
 
         def begin(self):
             for i in order:
                 for h in range(2):
-                    ref = self.piece(h, my, mx)
-                    self.first.append((i, h, self.send(ref, i, h, h, h * na + i - 1)))
+                    self.first(i, h).start()
             self.spread(0, 0)
             self.spread(0, 1)
 
         def spread(self, i, h):
-            yy = my if h == 0 else lax.rem(my + side - i, side)
-            xx = mx if h == 1 else lax.rem(mx + side - i, side)
-            ref = self.piece(h, yy, xx)
             for j in order:
-                n = 2 * na + (h * side + i) * na + j - 1
-                self.second.append(self.send(ref, j, h, 1 - h, n))
+                self.second(i, h, j).start()
 
         def forward(self):
-            for i, h, c in self.first:
-                c.wait_recv()
-                self.spread(i, h)
+            for i in order:
+                for h in range(2):
+                    self.first(i, h).wait_recv()
+                    self.spread(i, h)
 
         def finish(self):
-            for i, h, c in self.first:
-                c.wait_send()
-            for c in self.second:
-                c.wait()
+            for i in order:
+                for h in range(2):
+                    self.first(i, h).wait_send()
+            for i in range(side):
+                for h in range(2):
+                    for j in order:
+                        self.second(i, h, j).wait()
 
     cut = 2 * two + 128
     main = Gather(ag_v, a1_s, a1_r, ((0, cut), (cut, 2 * two)))
@@ -364,17 +372,18 @@
 
     dq = (jnp.dot(ds_, keys, preferred_element_type=F32) * factor).astype(BF16)
     for g in range(group):
-        dq_v[:, g * head:(g + 1) * head] = dq[g * seq:(g + 1) * seq, :]
-    dq_c = pltpu.make_async_copy(dq_v, dq_out, wr.at[0])
-    dq_c.start()
+        dq_out[:, g * head:(g + 1) * head] = dq[g * seq:(g + 1) * seq, :]
 
     main.forward()
     w_forward(2)
-    for c in n_sends[:len(offsets)]:
+    for c in n_sends:
         c.wait()
     main.finish()
-    extra.begin()
-    send_other(1)
+    @pl.when(pipe < n_pipe - 2)
+    def _():
+        extra.begin()
+        send_other(1)
+
 
     for q in range(w_pieces):
         w_arrived(2, q)
@@ -437,10 +446,16 @@
     def _():
         chain()
 
+    @pl.when(pipe >= n_pipe - 2)
+    def _():
+        extra.begin()
+        send_other(1)
+
     extra.forward()
 
-    for c in n_sends[len(offsets):]:
-        c.wait()
+    for p in range(2):
+        for c in others(p):
+            c.wait()
     extra.finish()
     nxt_own = nx_v[:, :, hi].reshape(tokens, blk).T
     nxt_oth = nx_v[:, :, oth].reshape(tokens, blk).T
@@ -466,20 +481,12 @@
         if dx or dy:
             deliver_copy(i).wait_recv()
         cc = blk_cols(at_xy(side - dx, side - dy))
-        so_v[:, cc] = (up_v[:, cc].astype(F32) + fr_v[i].astype(F32)).astype(BF16)
-    o = pltpu.make_async_copy(so_v, sc_out, wr.at[1])
-    o.start()
-    outs = [o]
+        sc_out[:, cc] = (up_v[:, cc].astype(F32) + fr_v[i].astype(F32)).astype(BF16)
 
     p_c.wait()
     tot = pw_v[lo] + pr_v[...].astype(F32)
-    kg_v[...] = tot[:, :head]
-    vg_v[...] = tot[:, head:]
-    kg_c = pltpu.make_async_copy(kg_v, kg_out, wr.at[1 + side])
-    vg_c = pltpu.make_async_copy(vg_v, vg_out, wr.at[2 + side])
-    kg_c.start()
-    vg_c.start()
-
+    kg_out[...] = tot[:, :head]
+    vg_out[...] = tot[:, head:]
     for i in range(n_dp):
         if i % side or dys[i // side]:
             deliver_copy(i).wait_send()
@@ -492,22 +499,12 @@
         for k in range(4):
             chain_copy(k).wait_send()
 
-    dq_c.wait()
-    for o in outs:
-        o.wait()
-    kg_c.wait()
-    vg_c.wait()
-
 
 def write_out(*refs):
     n = 4
-    ins, outs, bufs, sems = refs[:n], refs[n:2 * n], refs[2 * n:3 * n], refs[3 * n]
-    loads = [pltpu.make_async_copy(ins[i], bufs[i], sems.at[0, i]) for i in range(n)]
-    stores = [pltpu.make_async_copy(bufs[i], outs[i], sems.at[1, i]) for i in range(n)]
-    for c in loads:
-        c.start()
-    for c, o in zip(loads, stores):
-        c.wait()
+    ins, outs, sems = refs[:n], refs[n:2 * n], refs[2 * n]
+    stores = [pltpu.make_async_copy(ins[i], outs[i], sems.at[i]) for i in range(n)]
+    for o in stores:
         o.start()
     for o in stores:
         o.wait()
@@ -534,13 +531,13 @@
     sc, dq, kg, vg = pl.pallas_call(
         functools.partial(kernel, dims),
         out_shape=(
-            jax.ShapeDtypeStruct((quarter, width), BF16),
-            jax.ShapeDtypeStruct((seq, heads), BF16),
-            jax.ShapeDtypeStruct((blk, head), F32),
-            jax.ShapeDtypeStruct((blk, head), F32),
+            V((quarter, width), BF16),
+            V((seq, heads), BF16),
+            V((blk, head), F32),
+            V((blk, head), F32),
         ),
         in_specs=[any_spec] * 8,
-        out_specs=(any_spec,) * 4,
+        out_specs=(pl.BlockSpec(memory_space=V),) * 4,
         scratch_shapes=[
             V((seq, width), BF16),
             V((2, 2, quarter, width), BF16),
@@ -553,7 +550,6 @@
             V((1, width), F32),
             V((quarter, 128), F32),
             V((side, side, 2, quarter, blk), BF16),
-            V((seq, heads), BF16),
             V((seq, two), BF16),
             V((seq, 128), BF16),
             V((n_t, quarter, 128), BF16),
@@ -563,13 +559,10 @@
             V((n_dp, quarter, blk), BF16),
             V((side, side, quarter, blk), BF16),
             V((side, side, quarter, blk), BF16),
-            V((quarter, width), BF16),
             V((2, blk, two), F32),
             V((blk, two), BF16),
             V((blk, two), BF16),
-            V((blk, head), F32),
-            V((blk, head), F32),
-            DMA((19,)), DMA((3 + side,)),
+            DMA((19,)),
             DMA((8 * nz,)), DMA((8 * nz,)),
             DMA((3 * noff,)), DMA((3 * noff,)),
             DMA((n_t,)), DMA((n_t,)),
@@ -598,10 +591,10 @@
     sc, dq, kg, vg = pl.pallas_call(
         write_out,
         out_shape=tuple(jax.ShapeDtypeStruct(a.shape, a.dtype) for a in parts),
-        in_specs=[any_spec] * 4,
+        in_specs=[pl.BlockSpec(memory_space=V)] * 4,
         out_specs=(any_spec,) * 4,
-        scratch_shapes=[V(a.shape, a.dtype) for a in parts] + [DMA((2, 4))],
-        compiler_params=pltpu.CompilerParams(vmem_limit_bytes=62 << 20),
+        scratch_shapes=[DMA((4,))],
+        compiler_params=pltpu.CompilerParams(vmem_limit_bytes=16 << 20),
         name="write_out",
     )(*parts)
     return (

time: 60.2 us -> 57.1 us (0.949)
  Pallas kernels: 59.4 us -> 56.3 us
    pallas_call x1, Pallas kernels: 57.3 us -> 55.2 us  [per_device(): pl.pallas_call(functools.partial(kernel, dims), out_shape=(V((quarter, wi...]
    pallas_call x1, Pallas kernels: 2.16 us -> 1.09 us  [per_device(): pl.pallas_call(write_out, out_shape=tuple((jax.ShapeDtypeStruct(a.shape,...]
where the time goes in v4:
time: 57.1 us; the launch traced here: 57 us
  Pallas kernels  56.3 us (99%)
  between operations  0.64 us (1%)
    pallas_call x1, Pallas kernels, per_device(): pl.pallas_call(functools.partial(kernel, dims), out_shape=(V((quarter, wi...  55.2 us

profile of v4, /device:TPU:32, one launch (start us, length us, event | category | flops | bytes accessed | tf_op | source)
XLA Modules:
  0.0 57.0 jit_solution(7395691566928341139)
XLA Ops:
  0.6 55.2 %attention_backward.1 = (bf16[32,8192]{1,0:T(8,128)(2,1)S(1)}, bf16[128,1024]{1,0:T(8,128)(2,1)S(1)}, f32[512,128]{1,0:T(8,128)S(1)}, f32[512,128]{1,0:T(8,128)S(1)}) custom-call(bf16[128,8192]{1,0:T(8,128)(2,1)} %bitcast.11, f32[1,8192]{1,0:T(1,128)} %gain_hbm.1, bf16[8192,128]{1,0:T(8,128)(2,1)} %bitcast.12, bf16[8192,128]{1,0:T(8,128)(2,1)} %bitcast.13, ...), custom_call_target="tpu_custom_call" | custom-call | tf_op jit(solution)/shard_map/attention_backward/pallas_call | solution.py:531
  55.9 1.1 %write_out.1 = (bf16[32,8192]{1,0:T(8,128)(2,1)}, bf16[128,1024]{1,0:T(8,128)(2,1)}, f32[512,128]{1,0:T(8,128)}, f32[512,128]{1,0:T(8,128)}) custom-call(bf16[32,8192]{1,0:T(8,128)(2,1)S(1)} %get-tuple-element.12.refs_0_, bf16[128,1024]{1,0:T(8,128)(2,1)S(1)} %get-tuple-element.13.refs_1_, f32[512,128]{1,0:T(8,128)S(1)} %get-tuple-element.14.refs_2_, ...), custom_call_target="tpu_custom_call" | custom-call | tf_op jit(solution)/shard_map/write_out/pallas_call | solution.py:591

commit v5 on v4

--- a/solution.py
+++ b/solution.py
@@ -144,8 +144,8 @@
         ref = wg_v.at[pl.ds(q * prow, prow), cols]
         return remote(ref, ref, ws_s, ws_r, (r * w_pieces + q) * 2 + lane, dev_t(dev))
 
-    def w_round(r):
-        for q in range(w_pieces):
+    def w_round(r, pieces):
+        for q in pieces:
             @pl.when((t - r >= 0) & (t < n_t - 1))
             def _():
                 w_copy(0, r, q, t - r, t + 1).start()
@@ -184,7 +184,7 @@
             def _():
                 w_copy(1, r, q, t + r, t - 1).start()
 
-    w_round(0)
+    w_round(0, range(w_pieces // 2))
 
     gain_c.wait()
     x_cs[0].wait()
@@ -295,6 +295,7 @@
         c = remote(mp_v.at[r], mr_v.at[dt], zm_s, zm_r, dt - 1, dev_t(tt))
         c.start()
         m_sends.append(c)
+    w_round(0, range(w_pieces // 2, w_pieces))
     ag_v[my, mx, :, head_cols(t)] = dkv_v[own_rows, :]
     ax_v[my, mx, :, extra_cols(lo)] = dkv_v[rows_of(2), :]
     mr_v[0] = mp_v[own_rows, :]
@@ -394,8 +395,16 @@
     prev = (lax.rem(pipe + n_pipe - 1, n_pipe), d, t)
     dys = (2, 1, 3, 0)
 
-    def chain_copy(j):
-        return remote(sb_v.at[j], sr_v.at[j], c_s, c_r, j, prev)
+    def chain_copies(j):
+        return [remote(sb_v.at[j], sr_v.at[j], c_s, c_r, j, prev)]
+
+    def chain_send(j):
+        for c in chain_copies(j):
+            c.start()
+
+    def chain_take(j):
+        for c in chain_copies(j):
+            c.wait_recv()
 
     def deliver(j):
         dy = dys[j]
@@ -410,6 +419,15 @@
         dx, dy = i % side, dys[i // side]
         src = sb_v.at[i // side, lax.rem(mx + dx, side)]
         return remote(src, fr_v.at[i], g_s, g_r, i, dev_d(at_xy(dx, dy)))
+
+    def chain(j):
+        chain_take(j)
+        tot = cf_v[j] + sr_v[j].reshape(row, blk).astype(F32)
+        sb_v[j] = tot.astype(BF16).reshape(side, quarter, blk)
+
+        @pl.when(pipe > 0)
+        def _():
+            chain_send(j)
 
     for j, dy in enumerate(dys):
         yy = lax.rem(my + dy, side)
@@ -427,24 +445,21 @@
         @pl.when(pipe == n_pipe - 1)
         def _():
             sb_v[j] = con.astype(BF16).reshape(side, quarter, blk)
-            chain_copy(j).start()
+            chain_send(j)
+
+        if j:
+            @pl.when(pipe == n_pipe - 2)
+            def _():
+                chain(j - 1)
+
+    @pl.when(pipe == n_pipe - 2)
+    def _():
+        chain(side - 1)
+
+    @pl.when(pipe >= n_pipe - 2)
+    def _():
+        for j in range(side):
             deliver(j)
-
-    def chain():
-        for j in range(side):
-            chain_copy(j).wait_recv()
-            tot = cf_v[j] + sr_v[j].reshape(row, blk).astype(F32)
-            sb_v[j] = tot.astype(BF16).reshape(side, quarter, blk)
-
-            @pl.when(pipe > 0)
-            def _():
-                chain_copy(j).start()
-
-            deliver(j)
-
-    @pl.when(pipe == n_pipe - 2)
-    def _():
-        chain()
 
     @pl.when(pipe >= n_pipe - 2)
     def _():
@@ -473,7 +488,9 @@
 
     @pl.when(pipe < n_pipe - 2)
     def _():
-        chain()
+        for j in range(side):
+            chain(j)
+            deliver(j)
 
     up_c.wait()
     for i in range(n_dp):
@@ -496,8 +513,9 @@
 
     @pl.when(pipe > 0)
     def _():
-        for k in range(4):
-            chain_copy(k).wait_send()
+        for j in range(side):
+            for c in chain_copies(j):
+                c.wait_send()
 
 
 def write_out(*refs):
@@ -570,7 +588,7 @@
             DMA((na + side * na,)), DMA((na + side * na,)),
             DMA((na + side * na,)), DMA((na + side * na,)),
             DMA((n_dp,)), DMA((n_dp,)),
-            DMA((4,)), DMA((4,)),
+            DMA((n_dp,)), DMA((n_dp,)),
             DMA((1,)), DMA((1,)),
         ],
         compiler_params=pltpu.CompilerParams(

time: 57.1 us -> 54.5 us (0.954)
  Pallas kernels: 56.3 us -> 53.8 us
    pallas_call x1, Pallas kernels: 55.2 us -> 52.7 us  [per_device(): pl.pallas_call(functools.partial(kernel, dims), out_shape=(V((quarter, wi...]
where the time goes in v5:
time: 54.5 us; the launch traced here: 54.4 us
  Pallas kernels  53.8 us (99%)
  between operations  0.64 us (1%)
    pallas_call x1, Pallas kernels, per_device(): pl.pallas_call(functools.partial(kernel, dims), out_shape=(V((quarter, wi...  52.7 us

profile of v5, /device:TPU:32, one launch (start us, length us, event | category | flops | bytes accessed | tf_op | source)
XLA Modules:
  0.0 54.4 jit_solution(14303507079168544656)
XLA Ops:
  0.6 52.7 %attention_backward.1 = (bf16[32,8192]{1,0:T(8,128)(2,1)S(1)}, bf16[128,1024]{1,0:T(8,128)(2,1)S(1)}, f32[512,128]{1,0:T(8,128)S(1)}, f32[512,128]{1,0:T(8,128)S(1)}) custom-call(bf16[128,8192]{1,0:T(8,128)(2,1)} %bitcast.11, f32[1,8192]{1,0:T(1,128)} %gain_hbm.1, bf16[8192,128]{1,0:T(8,128)(2,1)} %bitcast.12, bf16[8192,128]{1,0:T(8,128)(2,1)} %bitcast.13, ...), custom_call_target="tpu_custom_call" | custom-call | tf_op jit(solution)/shard_map/attention_backward/pallas_call | solution.py:549
  53.3 1.1 %write_out.1 = (bf16[32,8192]{1,0:T(8,128)(2,1)}, bf16[128,1024]{1,0:T(8,128)(2,1)}, f32[512,128]{1,0:T(8,128)}, f32[512,128]{1,0:T(8,128)}) custom-call(bf16[32,8192]{1,0:T(8,128)(2,1)S(1)} %get-tuple-element.12.refs_0_, bf16[128,1024]{1,0:T(8,128)(2,1)S(1)} %get-tuple-element.13.refs_1_, f32[512,128]{1,0:T(8,128)S(1)} %get-tuple-element.14.refs_2_, ...), custom_call_target="tpu_custom_call" | custom-call | tf_op jit(solution)/shard_map/write_out/pallas_call | solution.py:609

commit v6 on v5

--- a/solution.py
+++ b/solution.py
@@ -136,7 +136,7 @@
         pl.semaphore_wait(barrier, peers)
 
     own_rows = rows_of(0)
-    w_pieces = 4
+    w_pieces = 2
     prow = blk // w_pieces
 
     def w_copy(lane, r, q, src, dev):

time: 54.5 us -> 54.5 us (level)
  no operation moved by 1% of the time
where the time goes in v6:
time: 54.5 us; the launch traced here: 54.4 us
  Pallas kernels  53.7 us (99%)
  between operations  0.64 us (1%)
    pallas_call x1, Pallas kernels, per_device(): pl.pallas_call(functools.partial(kernel, dims), out_shape=(V((quarter, wi...  52.7 us

profile of v6, /device:TPU:32, one launch (start us, length us, event | category | flops | bytes accessed | tf_op | source)
XLA Modules:
  0.0 54.4 jit_solution(7909473966097389893)
XLA Ops:
  0.6 52.7 %attention_backward.1 = (bf16[32,8192]{1,0:T(8,128)(2,1)S(1)}, bf16[128,1024]{1,0:T(8,128)(2,1)S(1)}, f32[512,128]{1,0:T(8,128)S(1)}, f32[512,128]{1,0:T(8,128)S(1)}) custom-call(bf16[128,8192]{1,0:T(8,128)(2,1)} %bitcast.11, f32[1,8192]{1,0:T(1,128)} %gain_hbm.1, bf16[8192,128]{1,0:T(8,128)(2,1)} %bitcast.12, bf16[8192,128]{1,0:T(8,128)(2,1)} %bitcast.13, ...), custom_call_target="tpu_custom_call" | custom-call | tf_op jit(solution)/shard_map/attention_backward/pallas_call | solution.py:549
  53.3 1.1 %write_out.1 = (bf16[32,8192]{1,0:T(8,128)(2,1)}, bf16[128,1024]{1,0:T(8,128)(2,1)}, f32[512,128]{1,0:T(8,128)}, f32[512,128]{1,0:T(8,128)}) custom-call(bf16[32,8192]{1,0:T(8,128)(2,1)S(1)} %get-tuple-element.12.refs_0_, bf16[128,1024]{1,0:T(8,128)(2,1)S(1)} %get-tuple-element.13.refs_1_, f32[512,128]{1,0:T(8,128)S(1)} %get-tuple-element.14.refs_2_, ...), custom_call_target="tpu_custom_call" | custom-call | tf_op jit(solution)/shard_map/write_out/pallas_call | solution.py:609

commit v7 on v5

--- a/solution.py
+++ b/solution.py
@@ -483,6 +483,16 @@
     for h in range(2):
         pw_v[h] = part[:, h * two:(h + 1) * two]
     ps_v[...] = pw_v[1 - lo].astype(BF16)
+
+    def chain_sent():
+        for j in range(side):
+            for c in chain_copies(j):
+                c.wait_send()
+
+    @pl.when(pipe >= n_pipe - 2)
+    def _():
+        chain_sent()
+
     p_c = remote(ps_v, pr_v, p_s, p_r, 0, dev_t(partner))
     p_c.start()
 
@@ -493,17 +503,25 @@
             deliver(j)
 
     up_c.wait()
-    for i in range(n_dp):
+
+    def finish_block(i):
         dx, dy = i % side, dys[i // side]
         if dx or dy:
             deliver_copy(i).wait_recv()
         cc = blk_cols(at_xy(side - dx, side - dy))
         sc_out[:, cc] = (up_v[:, cc].astype(F32) + fr_v[i].astype(F32)).astype(BF16)
 
+    for i in range(n_dp - side):
+        finish_block(i)
+
     p_c.wait()
     tot = pw_v[lo] + pr_v[...].astype(F32)
     kg_out[...] = tot[:, :head]
     vg_out[...] = tot[:, head:]
+
+    for i in range(n_dp - side, n_dp):
+        finish_block(i)
+
     for i in range(n_dp):
         if i % side or dys[i // side]:
             deliver_copy(i).wait_send()
@@ -511,11 +529,9 @@
         for q in range(w_pieces):
             w_sent(r, q)
 
-    @pl.when(pipe > 0)
-    def _():
-        for j in range(side):
-            for c in chain_copies(j):
-                c.wait_send()
+    @pl.when((pipe > 0) & (pipe < n_pipe - 2))
+    def _():
+        chain_sent()
 
 
 def write_out(*refs):

time: 54.5 us -> 54.6 us (level)
  no operation moved by 1% of the time
where the time goes in v7:
time: 54.6 us; the launch traced here: 54.3 us
  Pallas kernels  53.7 us (98%)
  between operations  0.64 us (1%)
    pallas_call x1, Pallas kernels, per_device(): pl.pallas_call(functools.partial(kernel, dims), out_shape=(V((quarter, wi...  52.6 us

profile of v7, /device:TPU:32, one launch (start us, length us, event | category | flops | bytes accessed | tf_op | source)
XLA Modules:
  0.0 54.3 jit_solution(4035498132941063842)
XLA Ops:
  0.6 52.6 %attention_backward.1 = (bf16[32,8192]{1,0:T(8,128)(2,1)S(1)}, bf16[128,1024]{1,0:T(8,128)(2,1)S(1)}, f32[512,128]{1,0:T(8,128)S(1)}, f32[512,128]{1,0:T(8,128)S(1)}) custom-call(bf16[128,8192]{1,0:T(8,128)(2,1)} %bitcast.11, f32[1,8192]{1,0:T(1,128)} %gain_hbm.1, bf16[8192,128]{1,0:T(8,128)(2,1)} %bitcast.12, bf16[8192,128]{1,0:T(8,128)(2,1)} %bitcast.13, ...), custom_call_target="tpu_custom_call" | custom-call | tf_op jit(solution)/shard_map/attention_backward/pallas_call | solution.py:565
  53.3 1.1 %write_out.1 = (bf16[32,8192]{1,0:T(8,128)(2,1)}, bf16[128,1024]{1,0:T(8,128)(2,1)}, f32[512,128]{1,0:T(8,128)}, f32[512,128]{1,0:T(8,128)}) custom-call(bf16[32,8192]{1,0:T(8,128)(2,1)S(1)} %get-tuple-element.12.refs_0_, bf16[128,1024]{1,0:T(8,128)(2,1)S(1)} %get-tuple-element.13.refs_1_, f32[512,128]{1,0:T(8,128)S(1)} %get-tuple-element.14.refs_2_, ...), custom_call_target="tpu_custom_call" | custom-call | tf_op jit(solution)/shard_map/write_out/pallas_call | solution.py:625
